TPU v7x, 128 devices: a whole 4x4x4 slice. The times are simulated.
128 devices in a mesh: row: 16 (over x_lo, z, core), col: 8 (over x_hi, y).
Axes of the slice: x: 4 (x_hi: 2, x_lo: 2; x = x_hi * 2 + x_lo), y: 4, z: 4, core: 2. Of those that a mesh axis runs over, the one named last changes fastest.
Arguments:
- pair: bfloat16 [512, 512, 128], P('row', 'col')
- valid_len: int32 [1], replicated, may hold values from 256 to 512
- tri_in: bfloat16 [128, 512], replicated, may hold values from -0.5 to 0.5
- tri_gate: bfloat16 [128, 128], replicated, may hold values from -0.5 to 0.5
- tri_out: bfloat16 [128, 128], replicated, may hold values from -0.5 to 0.5
- att_qkvg: bfloat16 [128, 512], replicated, may hold values from -0.5 to 0.5
- att_bias: bfloat16 [128, 4], replicated
- att_out: bfloat16 [128, 128], replicated, may hold values from -0.5 to 0.5
Outputs:
- updated: bfloat16 [512, 512, 128], P('row', 'col')
All inputs are finite; a program needn't handle non-finite values.
Results may differ from a plain program's by a relative error of at most 0.012.
Values may be sent and summed in bfloat16 or wider, within the bound.
A program may use at most 128 MiB of HBM per device.

v0:
```python
import math

import jax
import jax.numpy as jnp
from jax import lax
from jax.sharding import PartitionSpec as P


def spread(array, axis, root):
    mine = lax.axis_index(axis) == root
    return lax.psum(jnp.where(mine, array, jnp.zeros_like(array)), axis)


def layer_norm(values):
    mean = jnp.mean(values, axis=-1, keepdims=True)
    centred = values - mean
    var = jnp.mean(centred * centred, axis=-1, keepdims=True)
    return centred * lax.rsqrt(var + 1e-05)


def gated_product(proj, width, mask):
    return (jax.nn.sigmoid(proj[..., :width]) * proj[..., width:] * mask).astype(jnp.bfloat16)


def local(pair, valid_len, tri_in, tri_gate, tri_out, att_qkvg, att_bias, att_out):
    tile_rows, tile_cols, width = pair.shape
    hidden = tri_out.shape[0]
    heads = att_bias.shape[1]
    head_dim = width // heads
    scale = head_dim ** (-0.5)
    n_row = lax.axis_size("row")
    n_col = lax.axis_size("col")
    ratio = n_row // n_col
    row_id = lax.axis_index("row")
    col_id = lax.axis_index("col")
    limit = valid_len[0]
    rows_ok = row_id * tile_rows + jnp.arange(tile_rows) < limit
    cols_ok = col_id * tile_cols + jnp.arange(tile_cols) < limit
    pmask = (rows_ok[:, None] & cols_ok[None, :]).astype(jnp.float32)[..., None]
    pairf = pair.astype(jnp.float32)
    normed = layer_norm(pairf).astype(jnp.bfloat16)
    proj = jnp.dot(normed, tri_in, preferred_element_type=jnp.float32)
    left = gated_product(proj[..., : 2 * hidden], hidden, pmask)
    right = gated_product(proj[..., 2 * hidden :], hidden, pmask)
    right_rows = lax.all_gather(right, "col", axis=1, tiled=True)
    mirrored = []
    for offset in range(ratio):
        mirrored.append(spread(right_rows, "row", ratio * col_id + offset))
    right_mirror = jnp.concatenate(mirrored, axis=0)
    tgate = jax.nn.sigmoid(jnp.dot(normed, tri_gate, preferred_element_type=jnp.float32))
    product = jnp.einsum(
        "ikc,jkc->ijc",
        lax.all_gather(left, "col", axis=1, tiled=True),
        right_mirror,
        preferred_element_type=jnp.float32,
    )
    prodnorm = layer_norm(product).astype(jnp.bfloat16)
    first = (pairf + tgate * jnp.dot(prodnorm, tri_out, preferred_element_type=jnp.float32)).astype(
        jnp.bfloat16
    )
    firstf = first.astype(jnp.float32)
    second_norm = layer_norm(firstf).astype(jnp.bfloat16)
    bias_local = jnp.dot(second_norm, att_bias, preferred_element_type=jnp.float32).astype(
        jnp.bfloat16
    )
    qkvg = jnp.dot(second_norm, att_qkvg, preferred_element_type=jnp.float32)
    query = qkvg[..., :width].astype(jnp.bfloat16).reshape(tile_rows, tile_cols, heads, head_dim)
    key_value = qkvg[..., width : 3 * width].astype(jnp.bfloat16)
    agate = jax.nn.sigmoid(qkvg[..., 3 * width :])
    bias_rows = lax.all_gather(bias_local, "col", axis=1, tiled=True)
    bias_parts = []
    for offset in range(ratio):
        bias_parts.append(spread(bias_rows, "row", ratio * col_id + offset))
    bias_mirror = jnp.concatenate(bias_parts, axis=0)
    start_carry = (
        jnp.full((tile_rows, heads, tile_cols), -1e30, jnp.float32),
        jnp.zeros((tile_rows, heads, tile_cols), jnp.float32),
        jnp.zeros((tile_rows, heads, tile_cols, head_dim), jnp.float32),
    )
    kv_piece = lax.all_gather(key_value, "col", axis=1, tiled=True)
    length = kv_piece.shape[1]
    step = math.gcd(length, 128)
    count = length // step
    kv_blocks = jnp.moveaxis(kv_piece.reshape(tile_rows, count, step, 2 * width), 1, 0)
    bias_blocks = jnp.moveaxis(bias_mirror.reshape(tile_cols, count, step, heads), 1, 0)
    offsets = step * jnp.arange(count)

    def one_step(inner, items):
        running, summed, accum = inner
        kv_block, bias_block, begin = items
        keys = kv_block[..., :width].reshape(tile_rows, step, heads, head_dim)
        vals = kv_block[..., width:].reshape(tile_rows, step, heads, head_dim)
        bias_heads = jnp.transpose(bias_block, (2, 0, 1)).astype(jnp.float32)
        key_index = begin + jnp.arange(step)
        key_bias = jnp.where(key_index < limit, 0.0, -1000000000.0).astype(jnp.float32)
        scores = (
            jnp.einsum("ijhd,ikhd->ihjk", query, keys, preferred_element_type=jnp.float32) * scale
        )
        scores = scores + bias_heads[None] + key_bias
        newest = jnp.maximum(running, jnp.max(scores, axis=-1))
        expo = jnp.exp(scores - newest[..., None])
        factor = jnp.exp(running - newest)
        summed = summed * factor + jnp.sum(expo, axis=-1)
        accum = accum * factor[..., None] + jnp.einsum(
            "ihjk,ikhd->ihjd", expo.astype(jnp.bfloat16), vals, preferred_element_type=jnp.float32
        )
        return ((newest, summed, accum), None)

    result, unused = lax.scan(one_step, start_carry, (kv_blocks, bias_blocks, offsets))
    running, summed, accum = result
    att = jnp.transpose(accum / summed[..., None], (0, 2, 1, 3)).reshape(
        tile_rows, tile_cols, width
    )
    gated = (agate * att).astype(jnp.bfloat16)
    return (firstf + jnp.dot(gated, att_out, preferred_element_type=jnp.float32)).astype(
        jnp.bfloat16
    )


def solution(mesh):
    placed = (P("row", "col", None), P(), P(), P(), P(), P(), P(), P())
    return jax.shard_map(
        local, mesh=mesh, in_specs=placed, out_specs=P("row", "col", None), check_vma=False
    )
```

profile of v0, /device:TPU:1, one launch (start us, length us, event | category | flops | bytes accessed | tf_op | source)
XLA Modules:
  0.0 680.3 jit_solution(15308928567645027128)
XLA Ops:
  7.2 1.4 convert_reduce_fusion.1
  8.6 1.7 fusion.26
  10.4 2.0 fusion.45
  12.4 1.6 fusion.33
  14.1 0.7 all-gather.6.cloned.1.call-update
  14.8 73.4 %all-gather.4.cloned.1.call-done = bf16[32,512,128]{2,1,0:T(8,128)(2,1)} async-done(((bf16[32,64,128]{2,1,0:T(8,128)(2,1)}), bf16[32,512,128]{2,1,0:T(8,128)(2,1)}) %all-gather.4.cloned.1.call-update) | async-done | bytes 4194320 | tf_op jit(solution)/shard_map/all_gather | solution.py:45
  88.3 6.1 broadcast_select_fusion.1
  94.4 1.0 copy-done.4
  95.4 1.4 fusion.17
  96.8 63.0 %all-gather.6.cloned.1.call-done = bf16[32,512,128]{2,1,0:T(8,128)(2,1)} async-done(((bf16[32,64,128]{2,1,0:T(8,128)(2,1)}), bf16[32,512,128]{2,1,0:T(8,128)(2,1)}) %all-gather.6.cloned.1.call-update) | async-done | bytes 4194320 | tf_op jit(solution)/shard_map/all_gather | solution.py:53
  159.8 7.9 %copy.24 = bf16[32,512,128]{1,0,2:T(8,128)(2,1)} copy(bf16[32,512,128]{2,1,0:T(8,128)(2,1)} %all-gather.6.cloned.1.call-done) | data formatting | bytes 8388608 | tf_op jit(solution)/shard_map/all_gather | solution.py:53
  167.7 134.8 %all-reduce.7.cloned.1.call-done = (bf16[32,512,128]{2,1,0:T(8,128)(2,1)}, bf16[32,512,128]{2,1,0:T(8,128)(2,1)}) async-done(((bf16[32,512,128]{2,1,0:T(8,128)(2,1)}, bf16[32,512,128]{2,1,0:T(8,128)(2,1)}), (bf16[32,512,128]{2,1,0:T(8,128)(2,1)}, bf16[32,512,128]{2,1,0:T(8,128)(2,1)})) %all-reduce.7.cloned.1.call-update) | async-done | bytes 8388624 | tf_op jit(solution)/shard_map/psum | solution.py:11
  302.5 7.4 %pad_maximum_fusion = bf16[64,512,128]{2,1,0:T(8,128)(2,1)} fusion(bf16[32,512,128]{2,1,0:T(8,128)(2,1)} %get-tuple-element.114, bf16[32,512,128]{2,1,0:T(8,128)(2,1)} %get-tuple-element.115), kind=kLoop, calls=%fused_computation.21 | loop fusion | flops 4194304 | bytes 16777216 | tf_op jit(solution)/shard_map/concatenate | solution.py:49
  309.9 12.6 %copy.23 = bf16[64,512,128]{1,0,2:T(8,128)(2,1)} copy(bf16[64,512,128]{2,1,0:T(8,128)(2,1)} %pad_maximum_fusion) | data formatting | bytes 16777216 | tf_op jit(solution)/shard_map/concatenate | solution.py:49
  322.5 6.9 %bitcast_reduce_fusion = (f32[32,64]{1,0:T(8,128)S(1)}, f32[128,64,32]{1,2,0:T(8,128)S(1)}) fusion(bf16[64,512,128]{1,0,2:T(8,128)(2,1)} %copy.23, bf16[32,512,128]{1,0,2:T(8,128)(2,1)} %copy.24), kind=kOutput, calls=%fused_computation.25 | convolution fusion | flops 268695552 | bytes 13639680 | tf_op jit(solution)/shard_map/ikc,jkc->ijc/dot_general | solution.py:51
  329.5 0.3 multiply_reduce_fusion
  329.8 0.3 multiply_convert_fusion
  330.2 0.7 convert_reduce_fusion
  331.0 0.6 fusion.24
  331.6 0.7 convolution_convert_fusion
  332.5 28.5 %all_gather.15 = bf16[32,512,4]{0,2,1:T(4,128)(2,1)S(1)} all-gather(bf16[32,64,4]{0,2,1:T(4,128)(2,1)S(1)} %copy.28), channel_id=1, replica_groups=mesh['row'=16,'col'=8] {'col'}, dimensions={1}, use_global_device_ids=true | all-gather | bytes 147456 | tf_op jit(solution)/shard_map/all_gather | solution.py:70
  361.0 1.4 broadcast_select_fusion.3
  362.7 2.5 fusion.59
  365.2 1.3 copy-done.5
  366.5 1.1 slice.51
  367.6 1.1 slice.52
  368.7 1.3 copy.27
  370.1 118.0 %all-reduce.5.cloned.1.call-done = (bf16[32,512,4]{0,2,1:T(4,128)(2,1)}, bf16[32,512,4]{0,2,1:T(4,128)(2,1)}) async-done(((bf16[32,512,4]{0,2,1:T(4,128)(2,1)}, bf16[32,512,4]{0,2,1:T(4,128)(2,1)}), (bf16[32,512,4]{0,2,1:T(4,128)(2,1)}, bf16[32,512,4]{0,2,1:T(4,128)(2,1)})) %all-reduce.5.cloned.1.call-update) | async-done | bytes 262160 | tf_op jit(solution)/shard_map/psum | solution.py:11
  488.1 1.9 pad_maximum_fusion.1
  490.0 0.9 copy.29
  491.0 107.2 %all-gather.8.cloned.1.call-done = bf16[32,512,256]{2,1,0:T(8,128)(2,1)} async-done(((bf16[32,64,256]{2,1,0:T(8,128)(2,1)}), bf16[32,512,256]{2,1,0:T(8,128)(2,1)}) %all-gather.8.cloned.1.call-update) | async-done | bytes 8388624 | tf_op jit(solution)/shard_map/all_gather | solution.py:80
  598.2 11.9 %copy.26 = bf16[32,4,128,256]{2,3,0,1:T(8,128)(2,1)} copy(bf16[32,4,128,256]{3,2,1,0:T(8,128)(2,1)} %bitcast.96) | data formatting | bytes 16777216 | tf_op jit(solution)/shard_map/reshape | solution.py:84
  610.1 57.2 %while.15 = (s32[]{:T(128)}, f32[32,4,64]{2,1,0:T(4,128)S(1)}, f32[32,4,64]{2,1,0:T(4,128)S(1)}, f32[32,4,64,32]{2,3,1,0:T(8,128)S(1)}, bf16[4,32,128,256]{2,3,1...) while((s32[]{:T(128)}, f32[32,4,64]{2,1,0:T(4,128)S(1)}, ...), condition=%wide.region_13.14_spmd.clone, body=%wide.region_10.13_spmd.clone.sunk | while | flops 149758336 | bytes 45680844 | solution.py:109
  610.1 0.6 dynamic_slice.22
  610.7 1.2 compare_select_fusion.2
  611.9 0.9 convert_bitcast_fusion.2
  612.8 1.8 dynamic-slice_bitcast_fusion.2
  614.8 3.6 fusion.79
  618.4 4.1 fusion.80
  622.7 1.7 fusion.82
  624.4 0.6 dynamic_slice.22
  625.0 1.2 compare_select_fusion.2
  626.2 0.9 convert_bitcast_fusion.2
  627.1 1.8 dynamic-slice_bitcast_fusion.2
  629.1 3.6 fusion.79
  632.7 4.1 fusion.80
  637.0 1.7 fusion.82
  638.7 0.6 dynamic_slice.22
  639.3 1.2 compare_select_fusion.2
  640.5 0.9 convert_bitcast_fusion.2
  641.4 1.8 dynamic-slice_bitcast_fusion.2
  643.4 3.6 fusion.79
  647.0 4.1 fusion.80
  651.3 1.7 fusion.82
  653.0 0.6 dynamic_slice.22
  653.6 1.2 compare_select_fusion.2
  654.8 0.9 convert_bitcast_fusion.2
  655.7 1.8 dynamic-slice_bitcast_fusion.2
  657.7 3.6 fusion.79
  661.3 4.1 fusion.80
  665.6 1.7 fusion.82
  667.4 1.7 broadcast_divide_fusion
  669.0 2.2 copy.30
  671.3 2.4 fusion.19
  (73 shorter events, 1.9 us)
Async XLA Ops:
  6.5 356.1 %copy-start = (bf16[128,512]{1,0:T(8,128)(2,1)S(1)}, bf16[128,512]{1,0:T(8,128)(2,1)}, u32[]{:S(2)}) copy-start(bf16[128,512]{1,0:T(8,128)(2,1)} %param.15) | copy-start | bytes 393220
  6.5 81.7 %all-gather.4.cloned.1.call-start = ((), (), s32[]{:S(2)}) async-start(), calls=%async_computation | async-start | bytes 4718592 | tf_op jit(solution)/shard_map/all_gather | solution.py:45
  14.0 145.8 %all-gather.6.cloned.1.call-start = ((), (), s32[]{:S(2)}) async-start(), calls=%async_computation.1 | async-start | bytes 4718592 | tf_op jit(solution)/shard_map/all_gather | solution.py:53
  14.8 287.8 %all-reduce.7.cloned.1.call-start = ((), (), s32[]{:S(2)}) async-start(), calls=%async_computation.4 | async-start | bytes 16777216 | tf_op jit(solution)/shard_map/psum | solution.py:11
  94.4 1.0 copy-start.4
  94.4 1.0 copy-start.9
  94.4 393.7 %all-reduce.5.cloned.1.call-start = ((), (), s32[]{:S(2)}) async-start(), calls=%async_computation.3 | async-start | bytes 2097152 | tf_op jit(solution)/shard_map/psum | solution.py:11
  329.4 0.8 copy-start.8
  329.4 2.2 copy-start.11
  330.9 34.2 %copy-start.6 = (bf16[32,64,128]{2,1,0:T(8,128)(2,1)}, bf16[32,64,128]{2,1,0:T(8,128)(2,1)S(1)}, u32[]{:S(2)}) copy-start(bf16[32,64,128]{2,1,0:T(8,128)(2,1)S(1)} %get-tuple-element.131) | copy-start | bytes 1572868
  362.4 235.8 %all-gather.8.cloned.1.call-start = ((), (), s32[]{:S(2)}) async-start(), calls=%async_computation.2 | async-start | bytes 9437184 | tf_op jit(solution)/shard_map/all_gather | solution.py:80
  365.2 1.3 copy-start.5
  612.8 2.0 copy-start.3
  618.4 4.3 copy-start.2
  627.1 2.0 copy-start.3
  632.7 4.3 copy-start.2
  641.4 2.0 copy-start.3
  647.0 4.3 copy-start.2
  655.7 2.0 copy-start.3
  661.3 4.3 copy-start.2
  667.3 3.9 copy-start.7
  667.3 3.9 copy-start.10
  669.0 4.7 copy-start.1
Sparse Core Ops, SparseCore 0:
  14.1 74.0 all-gather.3
  90.6 69.1 all-gather.5
  162.4 140.1 all-reduce.6
  362.5 125.5 all-reduce.4
  490.5 107.6 all-gather.7
where the time goes:
time: 682 us; the launch traced here: 680 us
  waiting for transfers between devices  497 us (73%)
  local copies, waits for them, and re-layouts  51.9 us (8%)
  other arithmetic  49.8 us (7%)
  matrix products  37.8 us (6%)
  blocking collectives  28.5 us (4%)
  between operations  14.1 us (2%)
    psum x2, waiting for transfers between devices, spread(): return lax.psum(jnp.where(mine, array, jnp.zeros_like(array)), axis)  253 us
    all_gather x1, waiting for transfers between devices, local(): kv_piece = lax.all_gather(key_value, 'col', axis=1, tiled=True)  107 us
    all_gather x1, waiting for transfers between devices, local(): right_rows = lax.all_gather(right, 'col', axis=1, tiled=True)  73.4 us
    all_gather x1, waiting for transfers between devices, local(): lax.all_gather(left, 'col', axis=1, tiled=True)  63 us
    all_gather x1, blocking collectives, local(): bias_rows = lax.all_gather(bias_local, 'col', axis=1, tiled=True)  28.5 us
    reduce_sum x4, other arithmetic, one_step(): summed = summed * factor + jnp.sum(expo, axis=-1)  16.6 us
    dot_general x4, matrix products, one_step(): jnp.einsum('ijhd,ikhd->ihjk', query, keys, preferred_element_type=jnp.flo...  14.4 us
  transfers between devices with their start and end apart: 5, of which 5 were waited for; matrix products, arithmetic and copies ran while one was open for 4% of the time, Pallas kernels for 0%

commit v1 on v0

v1 whole, which is shorter than its diff:
```python
import functools

import jax
import jax.numpy as jnp
from jax import lax
from jax.experimental import pallas as pl
from jax.experimental.pallas import tpu as pltpu
from jax.sharding import PartitionSpec as P

MESH = pl.DeviceIdType.MESH


def layer_norm(values, axis):
    mean = jnp.mean(values, axis=axis, keepdims=True)
    centred = values - mean
    var = jnp.mean(centred * centred, axis=axis, keepdims=True)
    return centred * lax.rsqrt(var + 1e-05)


def place(whole, n_col, index):
    if whole:
        return (index // n_col, lax.rem(index, n_col))
    return (lax.axis_index("row"), index)


def exchange_kernel(n, n_col, whole, same, src, dst, send_sem, recv_sem, own_sem):
    me = lax.axis_index("col")
    if whole:
        me = lax.axis_index("row") * n_col + me
    barrier = pltpu.get_barrier_semaphore()

    def greet(step, carry):
        target = lax.rem(me + step, n)
        pl.semaphore_signal(
            barrier, inc=1, device_id=place(whole, n_col, target), device_id_type=MESH
        )
        return carry

    lax.fori_loop(1, n, greet, 0)
    pl.semaphore_wait(barrier, n - 1)
    own = pltpu.make_async_copy(src if same else src.at[me], dst.at[me], own_sem)
    own.start()

    def send(step, carry):
        target = lax.rem(me + step, n)
        pltpu.make_async_remote_copy(
            src_ref=src if same else src.at[target],
            dst_ref=dst.at[me],
            send_sem=send_sem,
            recv_sem=recv_sem,
            device_id=place(whole, n_col, target),
            device_id_type=MESH,
        ).start()
        return carry

    lax.fori_loop(1, n, send, 0)
    own.wait()
    others = dst.at[pl.ds(0, n - 1)]
    pltpu.make_async_copy(others, others, send_sem).wait()
    pltpu.make_async_copy(others, others, recv_sem).wait()


def exchange(array, n, n_col, collective_id, whole=True, same=False):
    shape = (n,) + array.shape if same else array.shape
    return pl.pallas_call(
        functools.partial(exchange_kernel, n, n_col, whole, same),
        out_shape=jax.ShapeDtypeStruct(shape, array.dtype),
        in_specs=[pl.BlockSpec(memory_space=pltpu.VMEM)],
        out_specs=pl.BlockSpec(memory_space=pltpu.VMEM),
        scratch_shapes=[pltpu.SemaphoreType.DMA] * 3,
        compiler_params=pltpu.CompilerParams(
            collective_id=collective_id, has_side_effects=True, vmem_limit_bytes=32 * 2**20
        ),
    )(array)


def local(pair, valid_len, tri_in, tri_gate, tri_out, att_qkvg, att_bias, att_out):
    tile_rows, tile_cols, width = pair.shape
    n_row, n_col = lax.axis_size("row"), lax.axis_size("col")
    n = n_row * n_col
    tokens = n_col * tile_cols
    own_rows = tokens // n
    heads = att_bias.shape[1]
    head_dim = width // heads
    limit = valid_len[0]
    keep = jnp.arange(tokens) < limit
    row_keep = lax.dynamic_slice(keep, (lax.axis_index("row") * tile_rows,), (tile_rows,))
    col_keep = lax.dynamic_slice(keep, (lax.axis_index("col") * tile_cols,), (tile_cols,))
    mask = (row_keep[:, None] & col_keep[None, :]).astype(jnp.float32)

    pair_rows = exchange(pair.reshape(n_col, own_rows, tile_cols, width), n_col, n_col, 0, whole=False)
    pair_rows = jnp.swapaxes(pair_rows, 0, 1).reshape(own_rows, tokens, width).astype(jnp.float32)

    normed = layer_norm(pair.astype(jnp.float32), -1).astype(jnp.bfloat16)
    proj = jnp.einsum("cd,ikc->dik", tri_in, normed, preferred_element_type=jnp.float32)
    proj = proj.reshape(4, width, tile_rows, tile_cols)
    left = (jax.nn.sigmoid(proj[0]) * proj[1] * mask).astype(jnp.bfloat16)
    right = (jax.nn.sigmoid(proj[2]) * proj[3] * mask).astype(jnp.bfloat16)
    both = jnp.stack([left, right], axis=1).reshape(n, 2, -1, 128)
    both = exchange(both, n, n_col, 1)
    both = both.reshape(n_row, n_col, 2, tile_rows, tile_cols)
    both = jnp.transpose(both, (2, 0, 3, 1, 4)).reshape(2, tokens, tokens)
    product = jnp.einsum("ik,jk->ij", both[0], both[1], preferred_element_type=jnp.float32)
    product = exchange(product.astype(jnp.bfloat16).reshape(n, -1, 128), n, n_col, 2)
    product = product.reshape(width, own_rows, tokens).astype(jnp.float32)
    prodnorm = layer_norm(product, 0).astype(jnp.bfloat16)

    normed = layer_norm(pair_rows, -1).astype(jnp.bfloat16)
    tgate = jax.nn.sigmoid(jnp.dot(normed, tri_gate, preferred_element_type=jnp.float32))
    update = jnp.einsum("cij,cd->ijd", prodnorm, tri_out, preferred_element_type=jnp.float32)
    first = (pair_rows + tgate * update).astype(jnp.bfloat16).astype(jnp.float32)
    normed = layer_norm(first, -1).astype(jnp.bfloat16)
    bias = jnp.einsum("jkc,ch->hjk", normed, att_bias, preferred_element_type=jnp.float32)
    bias = bias.astype(jnp.bfloat16).reshape(heads * own_rows, tokens)
    bias = exchange(bias, n, n_col, 3, same=True)
    bias = jnp.transpose(bias.reshape(n, heads, own_rows, tokens), (1, 0, 2, 3))
    bias = bias.reshape(heads, tokens, tokens).astype(jnp.float32)

    qkvg = jnp.dot(normed, att_qkvg, preferred_element_type=jnp.float32)
    agate = jax.nn.sigmoid(qkvg[..., 3 * width :])
    qkv = qkvg[..., : 3 * width].astype(jnp.bfloat16)
    qkv = qkv.reshape(own_rows, tokens, 3, heads, head_dim)
    query, key, value = qkv[:, :, 0], qkv[:, :, 1], qkv[:, :, 2]
    scores = jnp.einsum("ijhd,ikhd->ihjk", query, key, preferred_element_type=jnp.float32)
    key_bias = jnp.where(keep, 0.0, -1000000000.0).astype(jnp.float32)
    scores = scores * head_dim ** (-0.5) + bias + key_bias
    expo = jnp.exp(scores - jnp.max(scores, axis=-1, keepdims=True))
    total = jnp.sum(expo, axis=-1)
    att = jnp.einsum(
        "ihjk,ikhd->ijhd", expo.astype(jnp.bfloat16), value, preferred_element_type=jnp.float32
    )
    att = att / jnp.swapaxes(total, 1, 2)[..., None]
    gated = (agate * att.reshape(own_rows, tokens, width)).astype(jnp.bfloat16)
    updated = first + jnp.dot(gated, att_out, preferred_element_type=jnp.float32)
    updated = updated.astype(jnp.bfloat16).reshape(own_rows, n_col, tile_cols, width)
    updated = exchange(jnp.swapaxes(updated, 0, 1), n_col, n_col, 4, whole=False)
    return updated.reshape(tile_rows, tile_cols, width)


def solution(mesh):
    placed = (P("row", "col", None), P(), P(), P(), P(), P(), P(), P())
    return jax.shard_map(
        local, mesh=mesh, in_specs=placed, out_specs=P("row", "col", None), check_vma=False
    )
```

time: 682 us -> 165 us (0.24)
  waiting for transfers between devices: 497 us -> 0 us
  Pallas kernels: 0 us -> 103 us
  other arithmetic: 49.8 us -> 12.6 us
  blocking collectives: 28.5 us -> 0 us
  local copies, waits for them, and re-layouts: 51.9 us -> 28.8 us
  matrix products: 37.8 us -> 18.7 us
  between operations: 14.1 us -> 1.12 us
    psum x2 -> x0, waiting for transfers between devices: 253 us -> none  [spread(): return lax.psum(jnp.where(mine, array, jnp.zeros_like(array)), axis)]
    all_gather x3 -> x0, waiting for transfers between devices: 244 us -> none  [the longest x1 107 us: local(): kv_piece = lax.all_gather(key_value, 'col', axis=1, tiled=True)]
    pallas_call x0 -> x5, Pallas kernels: none -> 103 us  [exchange(): pl.pallas_call(functools.partial(exchange_kernel, n, n_col, whole, same),...]
    all_gather x1 -> x0, blocking collectives: 28.5 us -> none  [local(): bias_rows = lax.all_gather(bias_local, 'col', axis=1, tiled=True)]
    dot_general x13 -> x7, matrix products: 34 us -> 15.4 us  [the longest x1 6.12 us: local(): jnp.einsum('ijhd,ikhd->ihjk', query, key, preferred_element_type=jnp.floa...]
    convert_element_type x1 -> x6, local copies, waits for them, and re-layouts: 0.12 us -> 15.1 us  [the longest x3 14.6 us: local(): bias = bias.reshape(heads, tokens, tokens).astype(jnp.float32)]
    concatenate x1 -> x0, local copies, waits for them, and re-layouts: 12.6 us -> none  [local(): right_mirror = jnp.concatenate(mirrored, axis=0)]
    select_n x6 -> x1, other arithmetic: 12.3 us -> 0.01 us  [local(): key_bias = jnp.where(keep, 0.0, -1000000000.0).astype(jnp.float32)]
  transfers between devices with their start and end apart: 5 -> 0, of which waited for: 5 -> 0; matrix products, arithmetic and copies ran while one was open for 4% -> 0% of each run, Pallas kernels for 0% -> 0%
where the time goes in v1:
time: 165 us; the launch traced here: 164 us
  Pallas kernels  103 us (62%)
  local copies, waits for them, and re-layouts  28.8 us (17%)
  matrix products  18.7 us (11%)
  other arithmetic  12.6 us (8%)
    pallas_call x5, Pallas kernels, exchange(): pl.pallas_call(functools.partial(exchange_kernel, n, n_col, whole, same),...  103 us
    convert_element_type x3, local copies, waits for them, and re-layouts, local(): bias = bias.reshape(heads, tokens, tokens).astype(jnp.float32)  14.6 us
    dot_general x1, matrix products, local(): jnp.einsum('ijhd,ikhd->ihjk', query, key, preferred_element_type=jnp.floa...  6.12 us
    reduce_sum x1, other arithmetic, local(): total = jnp.sum(expo, axis=-1)  4.57 us
    unnamed x24, local copies, waits for them, and re-layouts  4.19 us
    dot_general x1, matrix products, local(): jnp.einsum('ihjk,ikhd->ijhd', expo.astype(jnp.bfloat16), value, preferred...  3.88 us

profile of v1, /device:TPU:1, one launch (start us, length us, event | category | flops | bytes accessed | tf_op | source)
XLA Modules:
  0.0 164.1 jit_solution(4605832421610589983)
XLA Ops:
  0.0 0.0 copy-start
  0.7 0.1 dynamic_slice.7
  0.8 0.1 dynamic_slice.6
  0.9 0.1 and.28
  1.0 0.1 and.25
  1.0 0.1 and.26
  1.1 1.4 convert_reduce_fusion.1
  2.5 1.7 %fusion.25 = f32[32,64]{1,0:T(8,128)S(1)} fusion(bf16[32,64,128]{2,1,0:T(8,128)(2,1)} %param.8, f32[32,64]{1,0:T(8,128)S(1)} %broadcast_multiply_fusion), kind=kLoop, calls=%fused_computation.33 | loop fusion | flops 1046528 | bytes 540672 | tf_op jit(solution)/shard_map/reduce_sum | solution.py:16
  4.2 0.0 copy-start.2
  4.3 1.0 copy-done.2
  5.3 13.8 %shard_map.82 = bf16[8,4,64,128]{3,2,1,0:T(8,128)(2,1)S(1)} custom-call(bf16[8,4,64,128]{3,2,1,0:T(8,128)(2,1)S(1)} %bitcast.98), custom_call_target="tpu_custom_call" | custom-call | tf_op jit(solution)/shard_map/pallas_call | solution.py:65
  19.1 0.4 fusion.37
  19.5 0.1 div.71
  19.6 0.7 multiply_reduce_fusion.1
  20.2 0.1 rsqrt.39
  20.3 0.1 convert_bitcast_fusion
  20.4 0.1 copy.55
  20.5 0.0 copy-start.4
  20.5 1.0 copy-done.4
  21.5 1.4 fusion.36
  22.9 2.0 %convolution_bitcast_fusion = f32[512,32,64]{0,2,1:T(8,128)S(1)} fusion(bf16[32,64,128]{2,1,0:T(8,128)(2,1)} %param.8, f32[32,64]{1,0:T(8,128)S(1)} %add_rsqrt_fusion, f32[32,64]{1,0:T(8,128)S(1)} %broadcast_multiply_fusion, bf16[128,512]{1,0:T(8,128)(2,1)S(1)} %copy-done), kind=kOutput, calls=%fused_computation.7 | convolution fusion | flops 269484032 | bytes 4866048 | tf_op jit(solution)/shard_map/cd,ikc->dik/dot_general | solution.py:95
  24.9 0.6 slice_multiply_fusion.1
  25.4 0.0 copy-start.7
  25.4 0.5 copy.59
  26.0 0.0 copy-start.8
  26.0 0.5 copy.60
  26.5 0.2 multiply_convert_fusion.2
  26.7 0.0 copy-start.10
  26.7 0.1 pad_maximum_fusion.src
  26.8 25.0 %shard_map.83 = bf16[128,2,16,128]{3,2,1,0:T(8,128)(2,1)S(1)} custom-call(bf16[128,2,16,128]{3,2,1,0:T(8,128)(2,1)S(1)} %pad_maximum_fusion.src), custom_call_target="tpu_custom_call" | custom-call | tf_op jit(solution)/shard_map/pallas_call | solution.py:65
  51.8 0.8 reshape.263
  52.7 2.4 %copy.90 = bf16[16,8,2,32,64]{4,1,3,0,2:T(8,128)(2,1)S(1)} copy(bf16[16,8,2,32,64]{4,3,2,1,0:T(8,128)(2,1)S(1)} %reshape.263) | data formatting | bytes 2097152 | tf_op jit(solution)/shard_map/reshape | solution.py:101
  55.1 1.2 fusion.56
  56.3 1.9 %squeeze.30 = bf16[512,512]{1,0:T(8,128)(2,1)S(1)} reshape(bf16[1,16,32,8,64]{4,3,2,1,0:T(8,128)(2,1)} %get-tuple-element.7) | data formatting | bytes 1048576 | tf_op jit(solution)/shard_map/squeeze | solution.py:103
  58.2 0.6 squeeze.29
  58.8 0.5 convolution_convert_fusion
  59.3 0.3 reshape.264.src
  59.6 18.0 %shard_map.84 = bf16[128,16,128]{2,1,0:T(8,128)(2,1)S(1)} custom-call(bf16[128,16,128]{2,1,0:T(8,128)(2,1)S(1)} %reshape.264.src), custom_call_target="tpu_custom_call" | custom-call | tf_op jit(solution)/shard_map/pallas_call | solution.py:65
  77.7 0.1 convert_reduce_fusion.2
  77.8 0.2 multiply_reduce_fusion
  78.0 0.4 copy.76
  78.5 0.6 fusion.34
  79.1 0.0 copy-start.6
  79.1 0.3 fusion.48
  79.4 1.6 convert_reduce_fusion
  81.0 0.6 fusion.23
  81.7 0.7 fusion.22
  82.5 36.0 %shard_map.85 = bf16[128,16,512]{2,1,0:T(8,128)(2,1)S(1)} custom-call(bf16[16,512]{1,0:T(8,128)(2,1)S(1)} %reshape.266.src), custom_call_target="tpu_custom_call" | custom-call | tf_op jit(solution)/shard_map/pallas_call | solution.py:65
  118.5 3.2 %reshape.275 = f32[128,4,4,512]{3,2,1,0:T(4,128)} reshape(bf16[128,16,512]{2,1,0:T(8,128)(2,1)S(1)} %shard_map.85) | data formatting | bytes 6291456 | tf_op jit(solution)/shard_map/convert_element_type | solution.py:117
  121.7 6.2 %copy.69 = f32[128,4,4,512]{3,1,2,0:T(4,128)} copy(f32[128,4,4,512]{3,2,1,0:T(4,128)} %reshape.275) | data formatting | bytes 8388608 | tf_op jit(solution)/shard_map/convert_element_type | solution.py:117
  127.8 5.3 %copy.70 = f32[4,512,512]{1,2,0:T(8,128)} copy(f32[4,512,512]{2,0,1:T(4,128)} %bitcast.101) | data formatting | bytes 8388608 | tf_op jit(solution)/shard_map/convert_element_type | solution.py:117
  133.1 2.0 %fusion.43 = f32[4,512,512]{1,2,0:T(8,128)S(1)} fusion(bf16[4,512,128]{2,1,0:T(8,128)(2,1)S(1)} %get-tuple-element.12, f32[4,512]{1,0:T(4,128)S(1)} %add_rsqrt_fusion.1, f32[4,512]{1,0:T(4,128)S(1)} %broadcast_multiply_fusion.1, bf16[128,512]{1,0:T(8,128)(2,1)S(1)} %copy-done.6), kind=kOutput, calls=%fused_computation.67 | convolution fusion | flops 269484032 | bytes 4866048 | tf_op jit(solution)/shard_map/dot_general | solution.py:119
  135.1 0.1 slice.57
  135.2 0.2 slice.89
  135.4 1.3 copy.78
  136.7 6.1 %fusion.2 = (f32[4,4,512]{2,1,0:T(4,128)S(1)}, f32[4,4,512,512]{2,3,1,0:T(8,128)S(1)}) fusion(f32[512]{0:T(512)S(1)} %broadcast_select_fusion, f32[4,512,512]{1,2,0:T(8,128)} %copy.70, bf16[4,512,3,4,32]{1,4,3,2,0:T(8,128)(2,1)S(1)} %bitcast.103), kind=kOutput, calls=%fused_computation.4 | convolution fusion | flops 285204480 | bytes 22054912 | tf_op jit(solution)/shard_map/ijhd,ikhd->ihjk/dot_general | solution.py:124
  142.8 4.6 %fusion = f32[4,4,512]{2,1,0:T(4,128)S(1)} fusion(f32[4,4,512,512]{2,3,1,0:T(8,128)S(1)} %get-tuple-element.14, f32[4,4,512]{2,1,0:T(4,128)S(1)} %get-tuple-element.13, f32[512]{0:T(512)S(1)} %broadcast_select_fusion, f32[4,512,512]{1,2,0:T(8,128)S(1)} %copy-done.3), kind=kLoop, calls=%fused_computation.2 | loop fusion | flops 20963328 | bytes 21039104 | tf_op jit(solution)/shard_map/reduce_sum | solution.py:128
  147.4 0.0 copy-start.9
  147.4 0.0 copy-start.1
  147.5 3.9 %fusion.19 = f32[4,512,4,32]{1,3,2,0:T(8,128)S(1)} fusion(f32[4,4,512,512]{2,3,1,0:T(8,128)S(1)} %get-tuple-element.14, f32[4,4,512]{2,1,0:T(4,128)S(1)} %get-tuple-element.13, f32[512]{0:T(512)S(1)} %broadcast_select_fusion, f32[4,512,512]{1,2,0:T(8,128)S(1)} %copy-done.3, bf16[4,512,3,4,32]{1,4,3,2,0:T(8,128)(2,1)S(1)} %bitcast.104, ...), kind=kOutput, calls=%fused_computation.28 | convolution fusion | flops 289669120 | bytes 22611968 | tf_op jit(solution)/shard_map/ihjk,ikhd->ijhd/dot_general | solution.py:129
  151.3 0.3 copy.72
  151.7 1.6 %fusion.13 = bf16[4,512,128]{2,1,0:T(8,128)(2,1)S(1)} fusion(bf16[4,512,128]{2,1,0:T(8,128)(2,1)S(1)} %get-tuple-element.12, f32[4,512,128]{2,1,0:T(8,128)S(1)} %copy.72, f32[4,512,128]{2,1,0:T(8,128)} %copy.78, bf16[128,128]{1,0:T(8,128)(2,1)S(1)} %copy-done.9), kind=kOutput, calls=%fused_computation.21 | convolution fusion | flops 69206016 | bytes 3178496 | tf_op jit(solution)/shard_map/dot_general | solution.py:134
  153.4 9.9 %shard_map.86 = bf16[8,4,64,128]{3,2,1,0:T(8,128)(2,1)S(1)} custom-call(bf16[8,4,64,128]{3,2,1,0:T(8,128)(2,1)S(1)} %bitcast.99), custom_call_target="tpu_custom_call" | custom-call | tf_op jit(solution)/shard_map/pallas_call | solution.py:65
  163.3 0.8 copy.94
  (29 shorter events, 0.2 us)
Async XLA Ops:
  0.0 22.9 %copy-start = (bf16[128,512]{1,0:T(8,128)(2,1)S(1)}, bf16[128,512]{1,0:T(8,128)(2,1)}, u32[]{:S(2)}) copy-start(bf16[128,512]{1,0:T(8,128)(2,1)} %param.10) | copy-start | bytes 393220
  4.2 1.0 copy-start.2
  20.5 1.0 copy-start.4
  25.4 53.6 %copy-start.7 = (bf16[128,128]{1,0:T(8,128)(2,1)S(1)}, bf16[128,128]{1,0:T(8,128)(2,1)}, u32[]{:S(2)}) copy-start(bf16[128,128]{1,0:T(8,128)(2,1)} %param.12) | copy-start | bytes 98308
  26.0 53.4 %copy-start.8 = (bf16[128,128]{1,0:T(8,128)(2,1)S(1)}, bf16[128,128]{1,0:T(8,128)(2,1)}, u32[]{:S(2)}) copy-start(bf16[128,128]{1,0:T(8,128)(2,1)} %param.11) | copy-start | bytes 98308
  26.7 55.0 %copy-start.10 = (bf16[128,4]{0,1:T(4,128)(2,1)S(1)}, bf16[128,4]{0,1:T(4,128)(2,1)}, u32[]{:S(2)}) copy-start(bf16[128,4]{0,1:T(4,128)(2,1)} %param.14) | copy-start | bytes 3076
  55.1 24.3 %copy-start.5 = (f32[4,8,64,128]{3,2,1,0:T(8,128)S(1)}, f32[4,8,64,128]{3,2,1,0:T(8,128)}, u32[]{:S(2)}) copy-start(f32[4,8,64,128]{3,2,1,0:T(8,128)} %copy-done.4) | copy-start | bytes 3145732
  79.1 54.0 %copy-start.6 = (bf16[128,512]{1,0:T(8,128)(2,1)S(1)}, bf16[128,512]{1,0:T(8,128)(2,1)}, u32[]{:S(2)}) copy-start(bf16[128,512]{1,0:T(8,128)(2,1)} %param.13) | copy-start | bytes 393220
  136.7 6.1 %copy-start.3 = (f32[4,512,512]{1,2,0:T(8,128)S(1)}, f32[4,512,512]{1,2,0:T(8,128)}, u32[]{:S(2)}) copy-start(f32[4,512,512]{1,2,0:T(8,128)} %copy.70) | copy-start | bytes 12582916
  147.4 4.2 %copy-start.9 = (bf16[128,128]{1,0:T(8,128)(2,1)S(1)}, bf16[128,128]{1,0:T(8,128)(2,1)}, u32[]{:S(2)}) copy-start(bf16[128,128]{1,0:T(8,128)(2,1)} %param.15) | copy-start | bytes 98308
  147.4 16.7 %copy-start.1 = (bf16[128,512]{1,0:T(8,128)(2,1)S(1)}, bf16[128,512]{1,0:T(8,128)(2,1)}, u32[]{:S(2)}) copy-start(bf16[128,512]{1,0:T(8,128)(2,1)} %param.10) | copy-start | bytes 393220

commit v2 on v1

v2 whole, which is shorter than its diff:
```python
import functools

import jax
import jax.numpy as jnp
from jax import lax
from jax.experimental import pallas as pl
from jax.experimental.pallas import tpu as pltpu
from jax.sharding import PartitionSpec as P

MESH = pl.DeviceIdType.MESH
BF16, F32 = jnp.bfloat16, jnp.float32
N_ROW, N_COL, N_DEV, N_CHIP = 16, 8, 128, 64
ROWS, COLS, OWN, HALF, C = 32, 64, 8, 256, 128
HEADS, DH = 4, 32


def layer_norm(values, axis=-1):
    mean = jnp.mean(values, axis=axis, keepdims=True)
    centred = values - mean
    var = jnp.mean(centred * centred, axis=axis, keepdims=True)
    return centred * lax.rsqrt(var + 1e-05)


def sigmoid(values):
    return 0.5 * jnp.tanh(0.5 * values) + 0.5


def dot(a, b):
    return jnp.dot(a, b, preferred_element_type=F32)


def dot_t(a, b):
    return lax.dot_general(a, b, (((1,), (1,)), ((), ())), preferred_element_type=F32)


def wait(ref, sem):
    pltpu.make_async_copy(ref, ref, sem).wait()


def kernel(
    pair_ref, limit_ref, tri_in_ref, tri_gate_ref, tri_out_ref, qkvg_ref, abias_ref, aout_ref,
    out_ref,
    pair_v, zn, wt, stage, amsg, abuf, amat, xmsg, xbuf, xs, prow, tg, z1, yn, bmsg, bbuf,
    qx, kb, vb, ag, att, omsg,
    load_sem, pair_sem, a_sem, x_sem, yn_sem, b_send, b_recv, o_sem,
):
    r, q = lax.axis_index("row"), lax.axis_index("col")
    me = r * N_COL + q
    core = lax.rem(r, 2)
    chip = (r // 2) * N_COL + q
    part = chip // (N_CHIP // 2)
    limit = limit_ref[0]

    def at(device):
        return (device // N_COL, lax.rem(device, N_COL))

    def post(src, dst, send, recv, row, col):
        here = jnp.logical_and(row == r, col == q)

        @pl.when(here)
        def _():
            pltpu.make_async_copy(src, dst, recv).start()

        @pl.when(jnp.logical_not(here))
        def _():
            pltpu.make_async_remote_copy(
                src_ref=src, dst_ref=dst, send_sem=send, recv_sem=recv,
                device_id=(row, col), device_id_type=MESH,
            ).start()

    load = pltpu.make_async_copy(pair_ref, pair_v, load_sem)
    load.start()
    barrier = pltpu.get_barrier_semaphore()

    def greet(step, carry):
        pl.semaphore_signal(
            barrier, inc=1, device_id=at(lax.rem(me + step, N_DEV)), device_id_type=MESH
        )
        return carry

    lax.fori_loop(1, N_DEV, greet, 0)
    wt[...] = tri_in_ref[...].T
    load.wait()

    def norm_block(b, carry):
        v = pair_v[pl.ds(4 * b, 4)].astype(F32)
        zn[pl.ds(4 * lax.rem(b, 4), 4), b // 4] = layer_norm(v).astype(BF16)
        return carry

    lax.fori_loop(0, 8, norm_block, 0)
    pl.semaphore_wait(barrier, N_DEV - 1)

    for u in range(4):
        owner = 4 * r + u
        post(
            pair_v.at[pl.ds(8 * u, 8)], prow.at[:, lax.rem(q, 4)], pair_sem.at[0], pair_sem.at[1],
            2 * (owner // N_COL) + q // 4, lax.rem(owner, N_COL),
        )

    s_id = lax.broadcasted_iota(jnp.int32, (16, 128), 0)
    l_id = lax.broadcasted_iota(jnp.int32, (16, 128), 1)
    i_id = ROWS * r + 16 * (l_id // COLS) + s_id
    k_id = COLS * q + lax.rem(l_id, COLS)
    mask = jnp.where((i_id < limit) & (k_id < limit), 1.0, 0.0).astype(F32)

    def send_ab(n, carry):
        first = 32 * lax.rem(me // 32 + n, 4)
        weights = jnp.concatenate(
            [wt[pl.ds(pl.multiple_of(k * C + first, 32), 32)] for k in range(4)], axis=0
        )

        def gate(piece, inner):
            rhs = zn[pl.ds(4 * piece, 4)].reshape(512, C)
            proj = dot_t(weights, rhs)
            a = sigmoid(proj[0:32]) * proj[32:64]
            b = sigmoid(proj[64:96]) * proj[96:128]
            for k in range(4):
                s = 4 * piece + k
                stage[pl.ds(s, 32, stride=32)] = a[:, 128 * k : 128 * (k + 1)]
                stage[pl.ds(16 + s, 32, stride=32)] = b[:, 128 * k : 128 * (k + 1)]
            return inner

        lax.fori_loop(0, 4, gate, 0)
        both = stage[...].reshape(32, 2, 16, 128) * mask
        amsg[pl.ds(first, 32)] = both.astype(BF16)

        def send(w, inner):
            to = first + lax.rem(me + w, 32)
            post(amsg.at[to], abuf.at[r, q], a_sem.at[0], a_sem.at[1], *at(to))
            return inner

        lax.fori_loop(0, 32, send, 0)
        return carry

    lax.fori_loop(0, 4, send_ab, 0)

    wait(prow, pair_sem.at[1])

    def tri_gate(s, carry):
        v = prow[s].reshape(HALF, C).astype(F32)
        tg[s] = sigmoid(dot(layer_norm(v).astype(BF16), tri_gate_ref[...]))
        return carry

    lax.fori_loop(0, OWN, tri_gate, 0)

    wait(abuf, a_sem.at[1])
    for side in range(2):
        for u in range(4):
            even = abuf[:, 2 * u, side].reshape(256, 128)
            odd = abuf[:, 2 * u + 1, side].reshape(256, 128)
            low = jnp.concatenate([even[:, :64], odd[:, :64]], axis=1).reshape(16, 1, 16, 128)
            high = jnp.concatenate([even[:, 64:], odd[:, 64:]], axis=1).reshape(16, 1, 16, 128)
            amat[side, :, 128 * u : 128 * (u + 1)] = jnp.concatenate([low, high], axis=1).reshape(
                512, 128
            )

    def send_x(n, carry):
        g = lax.rem(me // 32 + n, 4)
        x = dot_t(amat[0, pl.ds(pl.multiple_of(128 * g, 128), 128)], amat[1]).reshape(2, 8, 8, 512)
        for mm in range(2):
            for c in range(2):
                tiles = [x[mm, :, :, 128 * t : 128 * (t + 1)] for t in (2 * c, 2 * c + 1)]
                xmsg[4 * g + 2 * mm + c] = jnp.concatenate(tiles, axis=1).astype(BF16)

        def send(w, inner):
            to = at(32 * g + lax.rem(me + w, 32))
            post(xmsg.at[to[0], to[1]], xbuf.at[me], x_sem.at[0], x_sem.at[1], *to)
            return inner

        lax.fori_loop(0, 32, send, 0)
        return carry

    lax.fori_loop(0, 4, send_x, 0)

    wait(xbuf, x_sem.at[1])
    xs[...] = layer_norm(xbuf[...].astype(F32), 0).reshape(2048, 128)
    for p in range(16):
        s, t = p % 8, p // 8
        xn = xs[pl.ds(p, 128, stride=16)].T.astype(BF16)
        update = dot(xn, tri_out_ref[...])
        v = prow[s, 2 * t : 2 * t + 2].reshape(128, C).astype(F32)
        first = (v + tg[s, 128 * t : 128 * (t + 1)] * update).astype(BF16)
        z1[s, 128 * t : 128 * (t + 1)] = first
        yn[core, s, 128 * t : 128 * (t + 1)] = layer_norm(first.astype(F32)).astype(BF16)

    share = pltpu.make_async_remote_copy(
        src_ref=yn.at[core], dst_ref=yn.at[core], send_sem=yn_sem.at[0], recv_sem=yn_sem.at[1],
        device_id=(r + 1 - 2 * core, q), device_id_type=MESH,
    )
    share.start()

    place = lax.rem(lax.broadcasted_iota(jnp.int32, (32, C), 0), 8)
    bias = jnp.zeros((32, HALF), F32)
    for s in range(OWN):
        weights = jnp.where(place == s, abias_ref[...].astype(F32), 0.0).astype(BF16)
        bias += dot_t(weights, yn[core, s])
    bmsg[...] = bias.astype(BF16).reshape(2, 16, HALF)
    for pairing in range(2):

        def send_bias(w, carry, pairing=pairing):
            to = lax.rem(chip + w, N_CHIP)
            post(
                bmsg.at[pairing], bbuf.at[pairing, core, lax.rem(chip, N_CHIP // 2)],
                b_send.at[pairing], b_recv.at[pairing],
                2 * (to // N_COL) + part, lax.rem(to, N_COL),
            )
            return carry

        lax.fori_loop(0, N_CHIP, send_bias, 0)

    lane_head = lax.broadcasted_iota(jnp.int32, (8, C), 1) // DH

    def own_qkvg(s, carry):
        qkvg = dot(yn[core, s], qkvg_ref[...])
        query = (qkvg[:, :C] * DH ** (-0.5)).reshape(32, 1, 8, C)
        for pairing in range(2):
            rows = [jnp.where(lane_head == 2 * pairing + h, query, 0.0) for h in range(2)]
            qx[pairing, s] = jnp.concatenate(rows, axis=1).reshape(512, C).astype(BF16)
        kb[core, s] = qkvg[:, C : 2 * C].astype(BF16)
        vb[core, s] = qkvg[:, 2 * C : 3 * C].astype(BF16)
        ag[s] = sigmoid(qkvg[:, 3 * C :])
        return carry

    lax.fori_loop(0, OWN, own_qkvg, 0)
    share.wait()

    def other_kv(s, carry):
        kv = dot(yn[1 - core, s], qkvg_ref[:, C : 3 * C])
        kb[1 - core, s] = kv[:, :C].astype(BF16)
        vb[1 - core, s] = kv[:, C:].astype(BF16)
        return carry

    lax.fori_loop(0, OWN, other_kv, 0)

    key_id = lax.broadcasted_iota(jnp.int32, (1, 2 * HALF), 1)
    key_bias = jnp.where(key_id < limit, 0.0, -1000000000.0).astype(F32)

    def attend(pairing, s):
        keys = kb[:, s].reshape(2 * HALF, C)
        vals = vb[:, s].reshape(2 * HALF, C)
        bias = jnp.concatenate([bbuf[pairing, 0], bbuf[pairing, 1]], axis=-1)
        scores = dot_t(qx[pairing, s], keys) + (
            bias.reshape(512, 2 * HALF).astype(F32) + key_bias
        )
        expo = jnp.exp(scores - jnp.max(scores, axis=-1, keepdims=True))
        total = jnp.sum(expo, axis=-1, keepdims=True)
        got = (dot(expo.astype(BF16), vals) / total).reshape(32, 2, 8, C)
        part0 = jnp.where(lane_head == 2 * pairing, got[:, 0], 0.0)
        return jnp.where(lane_head == 2 * pairing + 1, got[:, 1], part0).reshape(HALF, C)

    wait(bbuf.at[0], b_recv.at[0])

    def first_heads(s, carry):
        att[s] = attend(0, s)
        return carry

    lax.fori_loop(0, OWN, first_heads, 0)
    wait(bbuf.at[1], b_recv.at[1])

    def last_heads(s, carry):
        gated = (ag[s] * (att[s] + attend(1, s))).astype(BF16)
        done = z1[s].astype(F32) + dot(gated, aout_ref[...])
        omsg[s] = done.astype(BF16).reshape(4, COLS, C)
        for u in range(4):
            post(
                omsg.at[s, u], out_ref.at[8 * lax.rem(chip, 4) + s], o_sem.at[0], o_sem.at[1],
                chip // 4, 4 * core + u,
            )
        return carry

    lax.fori_loop(0, OWN, last_heads, 0)

    wait(amsg.at[pl.ds(0, N_DEV - 1)], a_sem.at[0])
    wait(xbuf.at[pl.ds(0, N_DEV - 1)], x_sem.at[0])
    own_block = core == q // 4
    own_bias = core == part

    @pl.when(own_block)
    def _():
        wait(prow.at[pl.ds(0, 6)], pair_sem.at[0])
        wait(prow.at[pl.ds(0, 6)], o_sem.at[0])

    @pl.when(jnp.logical_not(own_block))
    def _():
        wait(prow, pair_sem.at[0])
        wait(prow, o_sem.at[0])

    @pl.when(own_bias)
    def _():
        for pairing in range(2):
            wait(bbuf.at[pairing, 0], b_send.at[pairing])
            wait(bbuf.at[pairing, 1, pl.ds(0, 31)], b_send.at[pairing])

    @pl.when(jnp.logical_not(own_bias))
    def _():
        for pairing in range(2):
            wait(bbuf.at[pairing], b_send.at[pairing])

    wait(out_ref, o_sem.at[1])


def local(pair, valid_len, tri_in, tri_gate, tri_out, att_qkvg, att_bias, att_out):
    bias_rows = jnp.repeat(att_bias.T, OWN, axis=0)
    vmem = pl.BlockSpec(memory_space=pltpu.VMEM)
    hbm = pl.BlockSpec(memory_space=pl.ANY)
    smem = pl.BlockSpec(memory_space=pltpu.SMEM)
    dma = pltpu.SemaphoreType.DMA
    return pl.pallas_call(
        kernel,
        out_shape=jax.ShapeDtypeStruct(pair.shape, pair.dtype),
        in_specs=[hbm, smem] + [vmem] * 6,
        out_specs=hbm,
        scratch_shapes=[
            pltpu.VMEM((ROWS, COLS, C), BF16),
            pltpu.VMEM((16, 2, COLS, C), BF16),
            pltpu.VMEM((4 * C, C), BF16),
            pltpu.VMEM((1024, 128), F32),
            pltpu.VMEM((N_DEV, 2, 16, 128), BF16),
            pltpu.VMEM((N_ROW, N_COL, 2, 16, 128), BF16),
            pltpu.VMEM((2, 512, 512), BF16),
            pltpu.VMEM((N_ROW, N_COL, 16, 128), BF16),
            pltpu.VMEM((N_DEV, 16, 128), BF16),
            pltpu.VMEM((2048, 128), F32),
            pltpu.VMEM((OWN, 4, COLS, C), BF16),
            pltpu.VMEM((OWN, HALF, C), F32),
            pltpu.VMEM((OWN, HALF, C), BF16),
            pltpu.VMEM((2, OWN, HALF, C), BF16),
            pltpu.VMEM((2, 16, HALF), BF16),
            pltpu.VMEM((2, 2, N_CHIP // 2, 16, HALF), BF16),
            pltpu.VMEM((2, OWN, 512, C), BF16),
            pltpu.VMEM((2, OWN, HALF, C), BF16),
            pltpu.VMEM((2, OWN, HALF, C), BF16),
            pltpu.VMEM((OWN, HALF, C), F32),
            pltpu.VMEM((OWN, HALF, C), F32),
            pltpu.VMEM((OWN, 4, COLS, C), BF16),
            dma,
            dma((2,)),
            dma((2,)),
            dma((2,)),
            dma((2,)),
            dma((2,)),
            dma((2,)),
            dma((2,)),
        ],
        compiler_params=pltpu.CompilerParams(
            collective_id=0, has_side_effects=True, vmem_limit_bytes=40 * 2**20
        ),
        name="pairformer",
    )(pair, valid_len, tri_in, tri_gate, tri_out, att_qkvg, bias_rows, att_out)


def solution(mesh):
    placed = (P("row", "col", None), P(), P(), P(), P(), P(), P(), P())
    return jax.shard_map(
        local, mesh=mesh, in_specs=placed, out_specs=P("row", "col", None), check_vma=False
    )
```

time: 165 us -> 84.2 us (0.51)
  Pallas kernels: 103 us -> 77.1 us
  local copies, waits for them, and re-layouts: 28.8 us -> 5.93 us
  matrix products: 18.7 us -> 0 us
  other arithmetic: 12.6 us -> 0 us
    pallas_call x5 -> x1, Pallas kernels: 103 us -> 77.1 us  [local(): pl.pallas_call(kernel, out_shape=jax.ShapeDtypeStruct(pair.shape, pair.dt...]
    dot_general x9 -> x0, matrix products: 18.7 us -> none  [the longest x1 6.12 us: local(): jnp.einsum('ijhd,ikhd->ihjk', query, key, preferred_element_type=jnp.floa...]
    convert_element_type x6 -> x0, local copies, waits for them, and re-layouts: 15.1 us -> none  [the longest x3 14.6 us: local(): bias = bias.reshape(heads, tokens, tokens).astype(jnp.float32)]
    reduce_sum x8 -> x0, other arithmetic: 9.64 us -> none  [the longest x1 4.57 us: local(): total = jnp.sum(expo, axis=-1)]
    reshape x6 -> x1, local copies, waits for them, and re-layouts: 3.97 us -> 0.01 us  [local(): bias_rows = jnp.repeat(att_bias.T, OWN, axis=0)]
    squeeze x2 -> x0, local copies, waits for them, and re-layouts: 2.5 us -> none  [the longest x1 1.89 us: local(): both[1]]
    convert_element_type x5 -> x0, other arithmetic: 2.29 us -> none  [the longest x1 1.4 us: local(): normed = layer_norm(pair_rows, -1).astype(jnp.bfloat16)]
    unnamed x24 -> x15, local copies, waits for them, and re-layouts: 4.19 us -> 5.93 us
where the time goes in v2:
time: 84.2 us; the launch traced here: 83.8 us
  Pallas kernels  77.1 us (92%)
  local copies, waits for them, and re-layouts  5.93 us (7%)
    pallas_call x1, Pallas kernels, local(): pl.pallas_call(kernel, out_shape=jax.ShapeDtypeStruct(pair.shape, pair.dt...  77.1 us
    unnamed x15, local copies, waits for them, and re-layouts  5.93 us

profile of v2, /device:TPU:1, one launch (start us, length us, event | category | flops | bytes accessed | tf_op | source)
XLA Modules:
  0.0 83.8 jit_solution(8890786790045713885)
XLA Ops:
  0.0 0.0 copy-start
  0.7 0.0 copy-done
  0.7 0.0 copy-start.1
  0.7 1.0 %copy-done.1 = bf16[32,64,128]{2,1,0:T(8,128)(2,1)S(1)} copy-done((bf16[32,64,128]{2,1,0:T(8,128)(2,1)S(1)}, bf16[32,64,128]{2,1,0:T(8,128)(2,1)}, u32[]{:S(2)}) %copy-start.1) | copy-done | bytes 524312
  1.7 0.0 copy-start.2
  1.7 0.9 %copy-done.2 = bf16[128,512]{1,0:T(8,128)(2,1)S(1)} copy-done((bf16[128,512]{1,0:T(8,128)(2,1)S(1)}, bf16[128,512]{1,0:T(8,128)(2,1)}, u32[]{:S(2)}) %copy-start.2) | copy-done | bytes 131096
  2.6 0.0 copy-start.3
  2.6 0.9 %copy-done.3 = bf16[128,512]{1,0:T(8,128)(2,1)S(1)} copy-done((bf16[128,512]{1,0:T(8,128)(2,1)S(1)}, bf16[128,512]{1,0:T(8,128)(2,1)}, u32[]{:S(2)}) %copy-start.3) | copy-done | bytes 131096
  3.5 0.0 copy-start.4
  3.5 0.8 copy-done.4
  4.3 0.0 copy-start.5
  4.3 0.8 copy-done.5
  5.1 0.0 copy-start.6
  5.1 0.8 copy-done.6
  5.8 77.1 %pairformer.1 = bf16[32,64,128]{2,1,0:T(8,128)(2,1)S(1)} custom-call(bf16[32,64,128]{2,1,0:T(8,128)(2,1)S(1)} %copy-done.1, s32[1]{0:T(128)S(6)} %copy.10.limit_ref, bf16[128,512]{1,0:T(8,128)(2,1)S(1)} %copy-done.2, bf16[128,128]{1,0:T(8,128)(2,1)S(1)} %copy-done.4, bf16[128,128]{1,0:T(8,128)(2,1)S(1)} %copy-done.5, bf16[128,512]{1,0:T(8,128)(2,1)S(1)} %copy-done.3, ...), custom_call_target="tpu_custom_call" | custom-call | tf_op jit(solution)/shard_map/pairformer/pallas_call | solution.py:308
  83.0 0.8 copy.11
  (1 shorter events, 0.0 us)
Async XLA Ops:
  0.0 0.7 copy-start
  0.7 1.0 %copy-start.1 = (bf16[32,64,128]{2,1,0:T(8,128)(2,1)S(1)}, bf16[32,64,128]{2,1,0:T(8,128)(2,1)}, u32[]{:S(2)}) copy-start(bf16[32,64,128]{2,1,0:T(8,128)(2,1)} %pair_ref.1) | copy-start | bytes 1572868
  1.7 0.9 %copy-start.2 = (bf16[128,512]{1,0:T(8,128)(2,1)S(1)}, bf16[128,512]{1,0:T(8,128)(2,1)}, u32[]{:S(2)}) copy-start(bf16[128,512]{1,0:T(8,128)(2,1)} %tri_in_ref.1) | copy-start | bytes 393220
  2.6 0.9 %copy-start.3 = (bf16[128,512]{1,0:T(8,128)(2,1)S(1)}, bf16[128,512]{1,0:T(8,128)(2,1)}, u32[]{:S(2)}) copy-start(bf16[128,512]{1,0:T(8,128)(2,1)} %qkvg_ref.1) | copy-start | bytes 393220
  3.5 0.8 copy-start.4
  4.3 0.8 copy-start.5
  5.1 0.8 copy-start.6

commit v3 on v2

--- a/solution.py
+++ b/solution.py
@@ -1,4 +1,4 @@
-import functools
+import itertools
 
 import jax
 import jax.numpy as jnp
@@ -33,13 +33,20 @@
     return lax.dot_general(a, b, (((1,), (1,)), ((), ())), preferred_element_type=F32)
 
 
+def far_first(cores):
+    ring = (0, 1, 2, 1)
+    steps = itertools.product(range(4), range(4), range(4), cores)
+    return sorted(steps, key=lambda d: -(ring[d[0]] + ring[d[1]] + ring[d[2]]))
+
+
 def wait(ref, sem):
     pltpu.make_async_copy(ref, ref, sem).wait()
 
 
 def kernel(
-    pair_ref, limit_ref, tri_in_ref, tri_gate_ref, tri_out_ref, qkvg_ref, abias_ref, aout_ref,
+    pair_ref, limit_ref, tri_in_hbm, tri_gate_hbm, tri_out_hbm, qkvg_hbm, abias_hbm, aout_hbm,
     out_ref,
+    tri_in_ref, tri_gate_ref, tri_out_ref, qkvg_ref, abias_ref, aout_ref,
     pair_v, zn, wt, stage, amsg, abuf, amat, xmsg, xbuf, xs, prow, tg, z1, yn, bmsg, bbuf,
     qx, kb, vb, ag, att, omsg,
     load_sem, pair_sem, a_sem, x_sem, yn_sem, b_send, b_recv, o_sem,
@@ -51,6 +58,23 @@
     part = chip // (N_CHIP // 2)
     limit = limit_ref[0]
 
+    cx, cy, cz = 2 * (q // 4) + r // 8, lax.rem(q, 4), lax.rem(r // 2, 4)
+    xs_at = [lax.rem(cx + d, 4) for d in range(4)]
+    ys_at = [lax.rem(cy + d, 4) for d in range(4)]
+    zs_at = [lax.rem(cz + d, 4) for d in range(4)]
+    core_at = [core, 1 - core]
+    quarter = lax.rem(cx + cy + cz, 4)
+    channel = 32 * quarter + 8 * cx + 2 * cy + core
+
+    def device(x, y, z, which):
+        return 8 * lax.rem(x, 2) + 2 * z + which, 4 * (x // 2) + y
+
+    def push(src, dst, send, recv, to):
+        pltpu.make_async_remote_copy(
+            src_ref=src, dst_ref=dst, send_sem=send, recv_sem=recv,
+            device_id=to, device_id_type=MESH,
+        ).start()
+
     def at(device):
         return (device // N_COL, lax.rem(device, N_COL))
 
@@ -68,8 +92,18 @@
                 device_id=(row, col), device_id_type=MESH,
             ).start()
 
-    load = pltpu.make_async_copy(pair_ref, pair_v, load_sem)
-    load.start()
+    loads = [
+        pltpu.make_async_copy(src, dst, load_sem.at[k])
+        for k, (src, dst) in enumerate(
+            [
+                (pair_ref, pair_v), (tri_in_hbm, tri_in_ref), (tri_gate_hbm, tri_gate_ref),
+                (tri_out_hbm, tri_out_ref), (qkvg_hbm, qkvg_ref), (abias_hbm, abias_ref),
+                (aout_hbm, aout_ref),
+            ]
+        )
+    ]
+    for load in loads:
+        load.start()
     barrier = pltpu.get_barrier_semaphore()
 
     def greet(step, carry):
@@ -79,8 +113,9 @@
         return carry
 
     lax.fori_loop(1, N_DEV, greet, 0)
+    for load in loads:
+        load.wait()
     wt[...] = tri_in_ref[...].T
-    load.wait()
 
     def norm_block(b, carry):
         v = pair_v[pl.ds(4 * b, 4)].astype(F32)
@@ -103,8 +138,12 @@
     k_id = COLS * q + lax.rem(l_id, COLS)
     mask = jnp.where((i_id < limit) & (k_id < limit), 1.0, 0.0).astype(F32)
 
+    planes = sorted(itertools.product(range(4), range(4)), key=lambda d: -(d[0] % 2 + d[1] % 2))
+
     def send_ab(n, carry):
-        first = 32 * lax.rem(me // 32 + n, 4)
+        ahead = lax.rem(n + 1, 4)
+        group = lax.rem(quarter + ahead, 4)
+        first = 32 * group
         weights = jnp.concatenate(
             [wt[pl.ds(pl.multiple_of(k * C + first, 32), 32)] for k in range(4)], axis=0
         )
@@ -124,12 +163,16 @@
         both = stage[...].reshape(32, 2, 16, 128) * mask
         amsg[pl.ds(first, 32)] = both.astype(BF16)
 
-        def send(w, inner):
-            to = first + lax.rem(me + w, 32)
-            post(amsg.at[to], abuf.at[r, q], a_sem.at[0], a_sem.at[1], *at(to))
-            return inner
-
-        lax.fori_loop(0, 32, send, 0)
+        for dx, dy in planes:
+            tx, ty = xs_at[dx], ys_at[dy]
+            tz = lax.rem(group + 8 - tx - ty, 4)
+            for c in range(2):
+                to = device(tx, ty, tz, core_at[c])
+                src = amsg.at[first + 8 * tx + 2 * ty + core_at[c]]
+                if (dx, dy, c) == (0, 0, 0):
+                    post(src, abuf.at[r, q], a_sem.at[0], a_sem.at[1], *to)
+                else:
+                    push(src, abuf.at[r, q], a_sem.at[0], a_sem.at[1], to)
         return carry
 
     lax.fori_loop(0, 4, send_ab, 0)
@@ -154,23 +197,20 @@
                 512, 128
             )
 
-    def send_x(n, carry):
-        g = lax.rem(me // 32 + n, 4)
+    def product(g, carry):
         x = dot_t(amat[0, pl.ds(pl.multiple_of(128 * g, 128), 128)], amat[1]).reshape(2, 8, 8, 512)
         for mm in range(2):
             for c in range(2):
                 tiles = [x[mm, :, :, 128 * t : 128 * (t + 1)] for t in (2 * c, 2 * c + 1)]
                 xmsg[4 * g + 2 * mm + c] = jnp.concatenate(tiles, axis=1).astype(BF16)
-
-        def send(w, inner):
-            to = at(32 * g + lax.rem(me + w, 32))
-            post(xmsg.at[to[0], to[1]], xbuf.at[me], x_sem.at[0], x_sem.at[1], *to)
-            return inner
-
-        lax.fori_loop(0, 32, send, 0)
-        return carry
-
-    lax.fori_loop(0, 4, send_x, 0)
+        return carry
+
+    lax.fori_loop(0, 4, product, 0)
+    pltpu.make_async_copy(xmsg.at[r, q], xbuf.at[channel], x_sem.at[1]).start()
+    for dx, dy, dz, c in far_first([0, 1]):
+        if (dx, dy, dz, c) != (0, 0, 0, 0):
+            to = device(xs_at[dx], ys_at[dy], zs_at[dz], core_at[c])
+            push(xmsg.at[to[0], to[1]], xbuf.at[channel], x_sem.at[0], x_sem.at[1], to)
 
     wait(xbuf, x_sem.at[1])
     xs[...] = layer_norm(xbuf[...].astype(F32), 0).reshape(2048, 128)
@@ -190,23 +230,37 @@
     share.start()
 
     place = lax.rem(lax.broadcasted_iota(jnp.int32, (32, C), 0), 8)
+    columns = abias_ref[...].astype(F32)
+    columns = jnp.concatenate(
+        [jnp.broadcast_to(columns[h : h + 1], (8, C)) for h in range(HEADS)], axis=0
+    )
     bias = jnp.zeros((32, HALF), F32)
     for s in range(OWN):
-        weights = jnp.where(place == s, abias_ref[...].astype(F32), 0.0).astype(BF16)
+        weights = jnp.where(place == s, columns, 0.0).astype(BF16)
         bias += dot_t(weights, yn[core, s])
     bmsg[...] = bias.astype(BF16).reshape(2, 16, HALF)
-    for pairing in range(2):
-
-        def send_bias(w, carry, pairing=pairing):
-            to = lax.rem(chip + w, N_CHIP)
-            post(
-                bmsg.at[pairing], bbuf.at[pairing, core, lax.rem(chip, N_CHIP // 2)],
-                b_send.at[pairing], b_recv.at[pairing],
-                2 * (to // N_COL) + part, lax.rem(to, N_COL),
-            )
-            return carry
-
-        lax.fori_loop(0, N_CHIP, send_bias, 0)
+    def send_bias(pairing):
+        dst = bbuf.at[pairing, core, lax.rem(chip, N_CHIP // 2)]
+        for dx, dy, dz, _ in far_first([0]):
+            to = device(xs_at[dx], ys_at[dy], zs_at[dz], part)
+            if (dx, dy, dz) == (0, 0, 0):
+                post(bmsg.at[pairing], dst, b_send.at[pairing], b_recv.at[pairing], *to)
+            else:
+                push(bmsg.at[pairing], dst, b_send.at[pairing], b_recv.at[pairing], to)
+
+    def bias_sent(pairing):
+        own_bias = core == part
+
+        @pl.when(own_bias)
+        def _():
+            wait(bbuf.at[pairing, 0], b_send.at[pairing])
+            wait(bbuf.at[pairing, 1, pl.ds(0, 31)], b_send.at[pairing])
+
+        @pl.when(jnp.logical_not(own_bias))
+        def _():
+            wait(bbuf.at[pairing], b_send.at[pairing])
+
+    send_bias(0)
 
     lane_head = lax.broadcasted_iota(jnp.int32, (8, C), 1) // DH
 
@@ -231,6 +285,8 @@
         return carry
 
     lax.fori_loop(0, OWN, other_kv, 0)
+    bias_sent(0)
+    send_bias(1)
 
     key_id = lax.broadcasted_iota(jnp.int32, (1, 2 * HALF), 1)
     key_bias = jnp.where(key_id < limit, 0.0, -1000000000.0).astype(F32)
@@ -273,8 +329,6 @@
     wait(amsg.at[pl.ds(0, N_DEV - 1)], a_sem.at[0])
     wait(xbuf.at[pl.ds(0, N_DEV - 1)], x_sem.at[0])
     own_block = core == q // 4
-    own_bias = core == part
-
     @pl.when(own_block)
     def _():
         wait(prow.at[pl.ds(0, 6)], pair_sem.at[0])
@@ -285,32 +339,26 @@
         wait(prow, pair_sem.at[0])
         wait(prow, o_sem.at[0])
 
-    @pl.when(own_bias)
-    def _():
-        for pairing in range(2):
-            wait(bbuf.at[pairing, 0], b_send.at[pairing])
-            wait(bbuf.at[pairing, 1, pl.ds(0, 31)], b_send.at[pairing])
-
-    @pl.when(jnp.logical_not(own_bias))
-    def _():
-        for pairing in range(2):
-            wait(bbuf.at[pairing], b_send.at[pairing])
-
+    bias_sent(1)
     wait(out_ref, o_sem.at[1])
 
 
 def local(pair, valid_len, tri_in, tri_gate, tri_out, att_qkvg, att_bias, att_out):
-    bias_rows = jnp.repeat(att_bias.T, OWN, axis=0)
-    vmem = pl.BlockSpec(memory_space=pltpu.VMEM)
-    hbm = pl.BlockSpec(memory_space=pl.ANY)
+    hbm = pl.BlockSpec(memory_space=pltpu.HBM)
     smem = pl.BlockSpec(memory_space=pltpu.SMEM)
     dma = pltpu.SemaphoreType.DMA
     return pl.pallas_call(
         kernel,
         out_shape=jax.ShapeDtypeStruct(pair.shape, pair.dtype),
-        in_specs=[hbm, smem] + [vmem] * 6,
+        in_specs=[hbm, smem] + [hbm] * 6,
         out_specs=hbm,
         scratch_shapes=[
+            pltpu.VMEM(tri_in.shape, BF16),
+            pltpu.VMEM(tri_gate.shape, BF16),
+            pltpu.VMEM(tri_out.shape, BF16),
+            pltpu.VMEM(att_qkvg.shape, BF16),
+            pltpu.VMEM(att_bias.shape[::-1], BF16),
+            pltpu.VMEM(att_out.shape, BF16),
             pltpu.VMEM((ROWS, COLS, C), BF16),
             pltpu.VMEM((16, 2, COLS, C), BF16),
             pltpu.VMEM((4 * C, C), BF16),
@@ -333,7 +381,7 @@
             pltpu.VMEM((OWN, HALF, C), F32),
             pltpu.VMEM((OWN, HALF, C), F32),
             pltpu.VMEM((OWN, 4, COLS, C), BF16),
-            dma,
+            dma((7,)),
             dma((2,)),
             dma((2,)),
             dma((2,)),
@@ -343,10 +391,10 @@
             dma((2,)),
         ],
         compiler_params=pltpu.CompilerParams(
-            collective_id=0, has_side_effects=True, vmem_limit_bytes=40 * 2**20
+            collective_id=0, has_side_effects=True, vmem_limit_bytes=63 * 2**20
         ),
         name="pairformer",
-    )(pair, valid_len, tri_in, tri_gate, tri_out, att_qkvg, bias_rows, att_out)
+    )(pair, valid_len, tri_in, tri_gate, tri_out, att_qkvg, att_bias.T, att_out)
 
 
 def solution(mesh):

time: 84.2 us -> 75 us (0.89)
  Pallas kernels: 77.1 us -> 72.3 us
  local copies, waits for them, and re-layouts: 5.93 us -> 1.87 us
    pallas_call x1, Pallas kernels: 77.1 us -> 72.3 us  [local(): pl.pallas_call(kernel, out_shape=jax.ShapeDtypeStruct(pair.shape, pair.dt...]
    unnamed x15 -> x1, local copies, waits for them, and re-layouts: 5.93 us -> 1.87 us
where the time goes in v3:
time: 75 us; the launch traced here: 74.9 us
  Pallas kernels  72.3 us (96%)
  local copies, waits for them, and re-layouts  1.87 us (2%)
    pallas_call x1, Pallas kernels, local(): pl.pallas_call(kernel, out_shape=jax.ShapeDtypeStruct(pair.shape, pair.dt...  72.3 us
    unnamed x1, local copies, waits for them, and re-layouts  1.87 us

profile of v3, /device:TPU:1, one launch (start us, length us, event | category | flops | bytes accessed | tf_op | source)
XLA Modules:
  0.0 74.9 jit_solution(3261711743810258185)
XLA Ops:
  0.7 72.3 %pairformer.1 = bf16[32,64,128]{2,1,0:T(8,128)(2,1)} custom-call(bf16[32,64,128]{2,1,0:T(8,128)(2,1)} %pair_ref.1, s32[1]{0:T(128)S(6)} %copy.10.limit_ref, bf16[128,512]{1,0:T(8,128)(2,1)} %tri_in_hbm.1, bf16[128,128]{1,0:T(8,128)(2,1)} %tri_gate_hbm.1, bf16[128,128]{1,0:T(8,128)(2,1)} %tri_out_hbm.1, bf16[128,512]{1,0:T(8,128)(2,1)} %qkvg_hbm.1, ...), custom_call_target="tpu_custom_call" | custom-call | tf_op jit(solution)/shard_map/pairformer/pallas_call | solution.py:350
  73.0 1.9 %copy.11 = bf16[32,64,128]{2,1,0:T(8,128)(2,1)} copy(bf16[32,64,128]{2,1,0:T(8,128)(2,1)} %pairformer.1) | data formatting | bytes 1048576

commit v4 on v3

--- a/solution.py
+++ b/solution.py
@@ -49,7 +49,7 @@
     tri_in_ref, tri_gate_ref, tri_out_ref, qkvg_ref, abias_ref, aout_ref,
     pair_v, zn, wt, stage, amsg, abuf, amat, xmsg, xbuf, xs, prow, tg, z1, yn, bmsg, bbuf,
     qx, kb, vb, ag, att, omsg,
-    load_sem, pair_sem, a_sem, x_sem, yn_sem, b_send, b_recv, o_sem,
+    load_sem, in_sem, pair_sem, a_sem, x_sem, yn_sem, b_send, b_recv, o_sem,
 ):
     r, q = lax.axis_index("row"), lax.axis_index("col")
     me = r * N_COL + q
@@ -105,32 +105,31 @@
     for load in loads:
         load.start()
     barrier = pltpu.get_barrier_semaphore()
-
-    def greet(step, carry):
-        pl.semaphore_signal(
-            barrier, inc=1, device_id=at(lax.rem(me + step, N_DEV)), device_id_type=MESH
-        )
-        return carry
-
-    lax.fori_loop(1, N_DEV, greet, 0)
+    mates = [(2 * (r // 2) + core_at[c], lax.rem(q + k, N_COL)) for c in range(2) for k in range(N_COL)]
+    peers = [(lax.rem(r + 2 * k, N_ROW), q) for k in range(1, N_ROW // 2)]
+    for to in mates[1:] + peers:
+        pl.semaphore_signal(barrier, inc=1, device_id=to, device_id_type=MESH)
     for load in loads:
         load.wait()
-    wt[...] = tri_in_ref[...].T
-
-    def norm_block(b, carry):
-        v = pair_v[pl.ds(4 * b, 4)].astype(F32)
-        zn[pl.ds(4 * lax.rem(b, 4), 4), b // 4] = layer_norm(v).astype(BF16)
-        return carry
-
-    lax.fori_loop(0, 8, norm_block, 0)
-    pl.semaphore_wait(barrier, N_DEV - 1)
-
+    pl.semaphore_wait(barrier, len(mates) - 1 + len(peers))
+    for to in peers:
+        pl.semaphore_signal(in_sem, inc=1, device_id=to, device_id_type=MESH)
     for u in range(4):
         owner = 4 * r + u
         post(
             pair_v.at[pl.ds(8 * u, 8)], prow.at[:, lax.rem(q, 4)], pair_sem.at[0], pair_sem.at[1],
             2 * (owner // N_COL) + q // 4, lax.rem(owner, N_COL),
         )
+
+    wt[...] = tri_in_ref[...].T
+
+    def norm_block(b, carry):
+        v = pair_v[pl.ds(4 * b, 4)].astype(F32)
+        zn[pl.ds(4 * lax.rem(b, 4), 4), b // 4] = layer_norm(v).astype(BF16)
+        return carry
+
+    lax.fori_loop(0, 8, norm_block, 0)
+    pl.semaphore_wait(in_sem, len(peers))
 
     s_id = lax.broadcasted_iota(jnp.int32, (16, 128), 0)
     l_id = lax.broadcasted_iota(jnp.int32, (16, 128), 1)
@@ -382,6 +381,7 @@
             pltpu.VMEM((OWN, HALF, C), F32),
             pltpu.VMEM((OWN, 4, COLS, C), BF16),
             dma((7,)),
+            pltpu.SemaphoreType.REGULAR,
             dma((2,)),
             dma((2,)),
             dma((2,)),

time: 75 us -> 71.7 us (0.956)
  Pallas kernels: 72.3 us -> 69 us
    pallas_call x1, Pallas kernels: 72.3 us -> 69 us  [local(): pl.pallas_call(kernel, out_shape=jax.ShapeDtypeStruct(pair.shape, pair.dt...]
where the time goes in v4:
time: 71.7 us; the launch traced here: 71.5 us
  Pallas kernels  69 us (96%)
  local copies, waits for them, and re-layouts  1.87 us (3%)
    pallas_call x1, Pallas kernels, local(): pl.pallas_call(kernel, out_shape=jax.ShapeDtypeStruct(pair.shape, pair.dt...  69 us
    unnamed x1, local copies, waits for them, and re-layouts  1.87 us

profile of v4, /device:TPU:1, one launch (start us, length us, event | category | flops | bytes accessed | tf_op | source)
XLA Modules:
  0.0 71.5 jit_solution(10405516475433334164)
XLA Ops:
  0.7 69.0 %pairformer.1 = bf16[32,64,128]{2,1,0:T(8,128)(2,1)} custom-call(bf16[32,64,128]{2,1,0:T(8,128)(2,1)} %pair_ref.1, s32[1]{0:T(128)S(6)} %copy.10.limit_ref, bf16[128,512]{1,0:T(8,128)(2,1)} %tri_in_hbm.1, bf16[128,128]{1,0:T(8,128)(2,1)} %tri_gate_hbm.1, bf16[128,128]{1,0:T(8,128)(2,1)} %tri_out_hbm.1, bf16[128,512]{1,0:T(8,128)(2,1)} %qkvg_hbm.1, ...), custom_call_target="tpu_custom_call" | custom-call | tf_op jit(solution)/shard_map/pairformer/pallas_call | solution.py:349
  69.6 1.9 %copy.11 = bf16[32,64,128]{2,1,0:T(8,128)(2,1)} copy(bf16[32,64,128]{2,1,0:T(8,128)(2,1)} %pairformer.1) | data formatting | bytes 1048576

commit v5 on v4

--- a/solution.py
+++ b/solution.py
@@ -48,7 +48,7 @@
     out_ref,
     tri_in_ref, tri_gate_ref, tri_out_ref, qkvg_ref, abias_ref, aout_ref,
     pair_v, zn, wt, stage, amsg, abuf, amat, xmsg, xbuf, xs, prow, tg, z1, yn, bmsg, bbuf,
-    qx, kb, vb, ag, att, omsg,
+    qx, kb, vb, ag, omsg,
     load_sem, in_sem, pair_sem, a_sem, x_sem, yn_sem, b_send, b_recv, o_sem,
 ):
     r, q = lax.axis_index("row"), lax.axis_index("col")
@@ -57,6 +57,7 @@
     chip = (r // 2) * N_COL + q
     part = chip // (N_CHIP // 2)
     limit = limit_ref[0]
+    flip = lax.rem(q, 4) // 2
 
     cx, cy, cz = 2 * (q // 4) + r // 8, lax.rem(q, 4), lax.rem(r // 2, 4)
     xs_at = [lax.rem(cx + d, 4) for d in range(4)]
@@ -114,12 +115,12 @@
     pl.semaphore_wait(barrier, len(mates) - 1 + len(peers))
     for to in peers:
         pl.semaphore_signal(in_sem, inc=1, device_id=to, device_id_type=MESH)
-    for u in range(4):
-        owner = 4 * r + u
-        post(
-            pair_v.at[pl.ds(8 * u, 8)], prow.at[:, lax.rem(q, 4)], pair_sem.at[0], pair_sem.at[1],
-            2 * (owner // N_COL) + q // 4, lax.rem(owner, N_COL),
-        )
+    for k in (6, 2, 5, 7, 3, 1, 4, 0):
+        col = lax.rem(q + k, N_COL)
+        slot = 4 * lax.rem(core + lax.rem(col, 4) // 2, 2)
+        src = pair_v.at[pl.ds(4 * col, 4)]
+        dst = prow.at[pl.ds(slot, 4), lax.rem(q, 4)]
+        post(src, dst, pair_sem.at[0], pair_sem.at[1], 2 * (r // 2) + q // 4, col)
 
     wt[...] = tri_in_ref[...].T
 
@@ -133,9 +134,15 @@
 
     s_id = lax.broadcasted_iota(jnp.int32, (16, 128), 0)
     l_id = lax.broadcasted_iota(jnp.int32, (16, 128), 1)
-    i_id = ROWS * r + 16 * (l_id // COLS) + s_id
     k_id = COLS * q + lax.rem(l_id, COLS)
-    mask = jnp.where((i_id < limit) & (k_id < limit), 1.0, 0.0).astype(F32)
+    quad = s_id // 4 + core * (1 - 2 * lax.rem(s_id // 4, 2))
+    quad = 2 * lax.rem(quad, 2) + quad // 2
+
+    def masked(s_order):
+        i_id = ROWS * r + 16 * (l_id // COLS) + s_order
+        return jnp.where((i_id < limit) & (k_id < limit), 1.0, 0.0).astype(F32)
+
+    mask = jnp.stack([masked(4 * quad + lax.rem(s_id, 4)), masked(s_id)])
 
     planes = sorted(itertools.product(range(4), range(4)), key=lambda d: -(d[0] % 2 + d[1] % 2))
 
@@ -152,10 +159,11 @@
             proj = dot_t(weights, rhs)
             a = sigmoid(proj[0:32]) * proj[32:64]
             b = sigmoid(proj[64:96]) * proj[96:128]
+            swapped = 2 * lax.rem(piece, 2) + piece // 2
+            place = 4 * (swapped + core * (1 - 2 * lax.rem(swapped, 2)))
             for k in range(4):
-                s = 4 * piece + k
-                stage[pl.ds(s, 32, stride=32)] = a[:, 128 * k : 128 * (k + 1)]
-                stage[pl.ds(16 + s, 32, stride=32)] = b[:, 128 * k : 128 * (k + 1)]
+                stage[pl.ds(place + k, 32, stride=32)] = a[:, 128 * k : 128 * (k + 1)]
+                stage[pl.ds(16 + 4 * piece + k, 32, stride=32)] = b[:, 128 * k : 128 * (k + 1)]
             return inner
 
         lax.fori_loop(0, 4, gate, 0)
@@ -186,15 +194,23 @@
     lax.fori_loop(0, OWN, tri_gate, 0)
 
     wait(abuf, a_sem.at[1])
+    top = lax.rem(lax.broadcasted_iota(jnp.int32, (1, 16, 128), 1), 8) < 4
     for side in range(2):
         for u in range(4):
             even = abuf[:, 2 * u, side].reshape(256, 128)
             odd = abuf[:, 2 * u + 1, side].reshape(256, 128)
-            low = jnp.concatenate([even[:, :64], odd[:, :64]], axis=1).reshape(16, 1, 16, 128)
-            high = jnp.concatenate([even[:, 64:], odd[:, 64:]], axis=1).reshape(16, 1, 16, 128)
-            amat[side, :, 128 * u : 128 * (u + 1)] = jnp.concatenate([low, high], axis=1).reshape(
-                512, 128
-            )
+            low = jnp.concatenate([even[:, :64], odd[:, :64]], axis=1)
+            high = jnp.concatenate([even[:, 64:], odd[:, 64:]], axis=1)
+            if side == 1:
+                tiles = [low.reshape(16, 1, 16, 128), high.reshape(16, 1, 16, 128)]
+            else:
+                tiles = []
+                for half in (low, high):
+                    half = half.astype(F32).reshape(8, 2, 16, 128)
+                    one, two = half[:, 0], half[:, 1]
+                    tiles.append(jnp.where(top, one, two).astype(BF16).reshape(8, 1, 16, 128))
+                    tiles.append(jnp.where(top, two, one).astype(BF16).reshape(8, 1, 16, 128))
+            amat[side, :, 128 * u : 128 * (u + 1)] = jnp.concatenate(tiles, axis=1).reshape(512, 128)
 
     def product(g, carry):
         x = dot_t(amat[0, pl.ds(pl.multiple_of(128 * g, 128), 128)], amat[1]).reshape(2, 8, 8, 512)
@@ -228,47 +244,60 @@
     )
     share.start()
 
-    place = lax.rem(lax.broadcasted_iota(jnp.int32, (32, C), 0), 8)
-    columns = abias_ref[...].astype(F32)
-    columns = jnp.concatenate(
-        [jnp.broadcast_to(columns[h : h + 1], (8, C)) for h in range(HEADS)], axis=0
-    )
+    row_id = lax.broadcasted_iota(jnp.int32, (32, C), 0)
+    slot_id = 4 * (row_id // 16) + lax.rem(row_id, 4)
+    head_id = lax.rem(row_id // 4, 4)
+    columns = jnp.zeros((32, C), F32)
+    for h in range(HEADS):
+        columns = jnp.where(head_id == h, abias_ref[h : h + 1, :].astype(F32), columns)
     bias = jnp.zeros((32, HALF), F32)
     for s in range(OWN):
-        weights = jnp.where(place == s, columns, 0.0).astype(BF16)
+        weights = jnp.where(slot_id == s, columns, 0.0).astype(BF16)
         bias += dot_t(weights, yn[core, s])
     bmsg[...] = bias.astype(BF16).reshape(2, 16, HALF)
-    def send_bias(pairing):
-        dst = bbuf.at[pairing, core, lax.rem(chip, N_CHIP // 2)]
+
+    def send_bias(block):
+        src = bmsg.at[lax.rem(block + flip, 2)]
+        dst = bbuf.at[block, core, lax.rem(chip, N_CHIP // 2)]
         for dx, dy, dz, _ in far_first([0]):
             to = device(xs_at[dx], ys_at[dy], zs_at[dz], part)
             if (dx, dy, dz) == (0, 0, 0):
-                post(bmsg.at[pairing], dst, b_send.at[pairing], b_recv.at[pairing], *to)
+                post(src, dst, b_send.at[block], b_recv.at[block], *to)
             else:
-                push(bmsg.at[pairing], dst, b_send.at[pairing], b_recv.at[pairing], to)
-
-    def bias_sent(pairing):
+                push(src, dst, b_send.at[block], b_recv.at[block], to)
+
+    def bias_sent(block):
         own_bias = core == part
 
         @pl.when(own_bias)
         def _():
-            wait(bbuf.at[pairing, 0], b_send.at[pairing])
-            wait(bbuf.at[pairing, 1, pl.ds(0, 31)], b_send.at[pairing])
+            wait(bbuf.at[block, 0], b_send.at[block])
+            wait(bbuf.at[block, 1, pl.ds(0, 31)], b_send.at[block])
 
         @pl.when(jnp.logical_not(own_bias))
         def _():
-            wait(bbuf.at[pairing], b_send.at[pairing])
+            wait(bbuf.at[block], b_send.at[block])
 
     send_bias(0)
 
-    lane_head = lax.broadcasted_iota(jnp.int32, (8, C), 1) // DH
+    sub_id = lax.broadcasted_iota(jnp.int32, (128, C), 0)
+    upper = lax.rem(sub_id, 8) < 4
+    lane_head = lax.broadcasted_iota(jnp.int32, (2, 8, C), 2) // DH
+    row_head = 2 * lax.broadcasted_iota(jnp.int32, (2, 8, C), 0) + (
+        lax.broadcasted_iota(jnp.int32, (2, 8, C), 1) // 4
+    )
+    head_mask = jnp.where(lane_head == row_head, 1.0, 0.0).astype(F32)
 
     def own_qkvg(s, carry):
         qkvg = dot(yn[core, s], qkvg_ref[...])
-        query = (qkvg[:, :C] * DH ** (-0.5)).reshape(32, 1, 8, C)
-        for pairing in range(2):
-            rows = [jnp.where(lane_head == 2 * pairing + h, query, 0.0) for h in range(2)]
-            qx[pairing, s] = jnp.concatenate(rows, axis=1).reshape(512, C).astype(BF16)
+        query = (qkvg[:, :C] * DH ** (-0.5)).reshape(4, 2, 32, C)
+        for block in range(2):
+            v = query[:, block].reshape(128, C)
+            down, up = pltpu.roll(v, 4, 0), pltpu.roll(v, 124, 0)
+            even = jnp.where(upper, v, down).reshape(16, 1, 1, 8, C)
+            odd = jnp.where(upper, up, v).reshape(16, 1, 1, 8, C)
+            rows = jnp.concatenate([even * head_mask, odd * head_mask], axis=1)
+            qx[block, s] = rows.reshape(512, C).astype(BF16)
         kb[core, s] = qkvg[:, C : 2 * C].astype(BF16)
         vb[core, s] = qkvg[:, 2 * C : 3 * C].astype(BF16)
         ag[s] = sigmoid(qkvg[:, 3 * C :])
@@ -290,48 +319,45 @@
     key_id = lax.broadcasted_iota(jnp.int32, (1, 2 * HALF), 1)
     key_bias = jnp.where(key_id < limit, 0.0, -1000000000.0).astype(F32)
 
-    def attend(pairing, s):
+    def attend(block, s):
         keys = kb[:, s].reshape(2 * HALF, C)
         vals = vb[:, s].reshape(2 * HALF, C)
-        bias = jnp.concatenate([bbuf[pairing, 0], bbuf[pairing, 1]], axis=-1)
-        scores = dot_t(qx[pairing, s], keys) + (
-            bias.reshape(512, 2 * HALF).astype(F32) + key_bias
-        )
+        bias = jnp.concatenate([bbuf[block, 0], bbuf[block, 1]], axis=-1)
+        scores = dot_t(qx[block, s], keys) + (bias.reshape(512, 2 * HALF).astype(F32) + key_bias)
         expo = jnp.exp(scores - jnp.max(scores, axis=-1, keepdims=True))
         total = jnp.sum(expo, axis=-1, keepdims=True)
-        got = (dot(expo.astype(BF16), vals) / total).reshape(32, 2, 8, C)
-        part0 = jnp.where(lane_head == 2 * pairing, got[:, 0], 0.0)
-        return jnp.where(lane_head == 2 * pairing + 1, got[:, 1], part0).reshape(HALF, C)
-
-    wait(bbuf.at[0], b_recv.at[0])
-
-    def first_heads(s, carry):
-        att[s] = attend(0, s)
-        return carry
-
-    lax.fori_loop(0, OWN, first_heads, 0)
-    wait(bbuf.at[1], b_recv.at[1])
-
-    def last_heads(s, carry):
-        gated = (ag[s] * (att[s] + attend(1, s))).astype(BF16)
-        done = z1[s].astype(F32) + dot(gated, aout_ref[...])
-        omsg[s] = done.astype(BF16).reshape(4, COLS, C)
-        for u in range(4):
-            post(
-                omsg.at[s, u], out_ref.at[8 * lax.rem(chip, 4) + s], o_sem.at[0], o_sem.at[1],
-                chip // 4, 4 * core + u,
-            )
-        return carry
-
-    lax.fori_loop(0, OWN, last_heads, 0)
+        got = (dot(expo.astype(BF16), vals) / total).reshape(16, 2, 2, 8, C) * head_mask
+        got = jnp.sum(got, axis=2)
+        even, odd = got[:, 0].reshape(128, C), got[:, 1].reshape(128, C)
+        even = even + pltpu.roll(even, 124, 0)
+        odd = odd + pltpu.roll(odd, 4, 0)
+        return jnp.where(upper, even, odd)
+
+    for block in range(2):
+        wait(bbuf.at[block], b_recv.at[block])
+
+        def finish(s, carry, block=block):
+            gate = ag[s].reshape(4, 2, 32, C)[:, block].reshape(128, C)
+            first = z1[s].reshape(4, 2, 32, C)[:, block].reshape(128, C)
+            gated = (gate * attend(block, s)).astype(BF16)
+            done = first.astype(F32) + dot(gated, aout_ref[...])
+            omsg[s, :, 32 * block : 32 * (block + 1)] = done.astype(BF16).reshape(4, 32, C)
+            side = lax.rem(s // 4 + flip, 2)
+            for u in range(4):
+                src = omsg.at[s, u, pl.ds(32 * block, 32)]
+                dst = out_ref.at[4 * q + lax.rem(s, 4), pl.ds(32 * block, 32)]
+                post(src, dst, o_sem.at[0], o_sem.at[1], 2 * (r // 2) + side, 4 * core + u)
+            return carry
+
+        lax.fori_loop(0, OWN, finish, 0)
 
     wait(amsg.at[pl.ds(0, N_DEV - 1)], a_sem.at[0])
     wait(xbuf.at[pl.ds(0, N_DEV - 1)], x_sem.at[0])
     own_block = core == q // 4
     @pl.when(own_block)
     def _():
-        wait(prow.at[pl.ds(0, 6)], pair_sem.at[0])
-        wait(prow.at[pl.ds(0, 6)], o_sem.at[0])
+        wait(prow.at[pl.ds(0, 7)], pair_sem.at[0])
+        wait(prow.at[pl.ds(0, 7)], o_sem.at[0])
 
     @pl.when(jnp.logical_not(own_block))
     def _():
@@ -378,7 +404,6 @@
             pltpu.VMEM((2, OWN, HALF, C), BF16),
             pltpu.VMEM((2, OWN, HALF, C), BF16),
             pltpu.VMEM((OWN, HALF, C), F32),
-            pltpu.VMEM((OWN, HALF, C), F32),
             pltpu.VMEM((OWN, 4, COLS, C), BF16),
             dma((7,)),
             pltpu.SemaphoreType.REGULAR,

time: 71.7 us -> 69.5 us (0.969)
  Pallas kernels: 69 us -> 66.8 us
    pallas_call x1, Pallas kernels: 69 us -> 66.8 us  [local(): pl.pallas_call(kernel, out_shape=jax.ShapeDtypeStruct(pair.shape, pair.dt...]
where the time goes in v5:
time: 69.5 us; the launch traced here: 69.3 us
  Pallas kernels  66.8 us (96%)
  local copies, waits for them, and re-layouts  1.87 us (3%)
    pallas_call x1, Pallas kernels, local(): pl.pallas_call(kernel, out_shape=jax.ShapeDtypeStruct(pair.shape, pair.dt...  66.8 us
    unnamed x1, local copies, waits for them, and re-layouts  1.87 us

profile of v5, /device:TPU:1, one launch (start us, length us, event | category | flops | bytes accessed | tf_op | source)
XLA Modules:
  0.0 69.3 jit_solution(5101250869428829250)
XLA Ops:
  0.7 66.8 %pairformer.1 = bf16[32,64,128]{2,1,0:T(8,128)(2,1)} custom-call(bf16[32,64,128]{2,1,0:T(8,128)(2,1)} %pair_ref.1, s32[1]{0:T(128)S(6)} %copy.10.limit_ref, bf16[128,512]{1,0:T(8,128)(2,1)} %tri_in_hbm.1, bf16[128,128]{1,0:T(8,128)(2,1)} %tri_gate_hbm.1, bf16[128,128]{1,0:T(8,128)(2,1)} %tri_out_hbm.1, bf16[128,512]{1,0:T(8,128)(2,1)} %qkvg_hbm.1, ...), custom_call_target="tpu_custom_call" | custom-call | tf_op jit(solution)/shard_map/pairformer/pallas_call | solution.py:375
  67.4 1.9 %copy.11 = bf16[32,64,128]{2,1,0:T(8,128)(2,1)} copy(bf16[32,64,128]{2,1,0:T(8,128)(2,1)} %pairformer.1) | data formatting | bytes 1048576

commit v6 on v5

--- a/solution.py
+++ b/solution.py
@@ -48,7 +48,7 @@
     out_ref,
     tri_in_ref, tri_gate_ref, tri_out_ref, qkvg_ref, abias_ref, aout_ref,
     pair_v, zn, wt, stage, amsg, abuf, amat, xmsg, xbuf, xs, prow, tg, z1, yn, bmsg, bbuf,
-    qx, kb, vb, ag, omsg,
+    qx, kb, vb, ag, omsg, full_bias, raw,
     load_sem, in_sem, pair_sem, a_sem, x_sem, yn_sem, b_send, b_recv, o_sem,
 ):
     r, q = lax.axis_index("row"), lax.axis_index("col")
@@ -212,15 +212,12 @@
                     tiles.append(jnp.where(top, two, one).astype(BF16).reshape(8, 1, 16, 128))
             amat[side, :, 128 * u : 128 * (u + 1)] = jnp.concatenate(tiles, axis=1).reshape(512, 128)
 
-    def product(g, carry):
-        x = dot_t(amat[0, pl.ds(pl.multiple_of(128 * g, 128), 128)], amat[1]).reshape(2, 8, 8, 512)
-        for mm in range(2):
-            for c in range(2):
-                tiles = [x[mm, :, :, 128 * t : 128 * (t + 1)] for t in (2 * c, 2 * c + 1)]
-                xmsg[4 * g + 2 * mm + c] = jnp.concatenate(tiles, axis=1).astype(BF16)
-        return carry
-
-    lax.fori_loop(0, 4, product, 0)
+    x = dot_t(amat[0], amat[1]).reshape(8, 8, 8, 512)
+    for m in range(8):
+        for c in range(2):
+            tiles = [x[m, :, :, 128 * t : 128 * (t + 1)] for t in (2 * c, 2 * c + 1)]
+            xmsg[2 * m + c] = jnp.concatenate(tiles, axis=1).astype(BF16)
+
     pltpu.make_async_copy(xmsg.at[r, q], xbuf.at[channel], x_sem.at[1]).start()
     for dx, dy, dz, c in far_first([0, 1]):
         if (dx, dy, dz, c) != (0, 0, 0, 0):
@@ -229,56 +226,56 @@
 
     wait(xbuf, x_sem.at[1])
     xs[...] = layer_norm(xbuf[...].astype(F32), 0).reshape(2048, 128)
-    for p in range(16):
-        s, t = p % 8, p // 8
-        xn = xs[pl.ds(p, 128, stride=16)].T.astype(BF16)
-        update = dot(xn, tri_out_ref[...])
-        v = prow[s, 2 * t : 2 * t + 2].reshape(128, C).astype(F32)
-        first = (v + tg[s, 128 * t : 128 * (t + 1)] * update).astype(BF16)
-        z1[s, 128 * t : 128 * (t + 1)] = first
-        yn[core, s, 128 * t : 128 * (t + 1)] = layer_norm(first.astype(F32)).astype(BF16)
-
-    share = pltpu.make_async_remote_copy(
-        src_ref=yn.at[core], dst_ref=yn.at[core], send_sem=yn_sem.at[0], recv_sem=yn_sem.at[1],
-        device_id=(r + 1 - 2 * core, q), device_id_type=MESH,
-    )
-    share.start()
-
-    row_id = lax.broadcasted_iota(jnp.int32, (32, C), 0)
-    slot_id = 4 * (row_id // 16) + lax.rem(row_id, 4)
-    head_id = lax.rem(row_id // 4, 4)
-    columns = jnp.zeros((32, C), F32)
+    row_id = lax.broadcasted_iota(jnp.int32, (16, C), 0)
+    columns = jnp.zeros((16, C), F32)
     for h in range(HEADS):
-        columns = jnp.where(head_id == h, abias_ref[h : h + 1, :].astype(F32), columns)
-    bias = jnp.zeros((32, HALF), F32)
-    for s in range(OWN):
-        weights = jnp.where(slot_id == s, columns, 0.0).astype(BF16)
-        bias += dot_t(weights, yn[core, s])
-    bmsg[...] = bias.astype(BF16).reshape(2, 16, HALF)
-
-    def send_bias(block):
-        src = bmsg.at[lax.rem(block + flip, 2)]
-        dst = bbuf.at[block, core, lax.rem(chip, N_CHIP // 2)]
+        columns = jnp.where(row_id // 4 == h, abias_ref[h : h + 1, :].astype(F32), columns)
+    x_hi = cx // 2
+
+    def spread(block):
+        dst = bbuf.at[block, :, core, cz, x_hi, cy]
         for dx, dy, dz, _ in far_first([0]):
             to = device(xs_at[dx], ys_at[dy], zs_at[dz], part)
             if (dx, dy, dz) == (0, 0, 0):
-                post(src, dst, b_send.at[block], b_recv.at[block], *to)
+                post(bmsg.at[block], dst, b_send.at[block], b_recv.at[block], *to)
             else:
-                push(src, dst, b_send.at[block], b_recv.at[block], to)
-
-    def bias_sent(block):
-        own_bias = core == part
-
-        @pl.when(own_bias)
+                push(bmsg.at[block], dst, b_send.at[block], b_recv.at[block], to)
+
+    def spread_done(block):
+        @pl.when(core == part)
         def _():
-            wait(bbuf.at[block, 0], b_send.at[block])
-            wait(bbuf.at[block, 1, pl.ds(0, 31)], b_send.at[block])
-
-        @pl.when(jnp.logical_not(own_bias))
+            wait(bbuf.at[block, :, 0], b_send.at[block])
+            wait(bbuf.at[block, :, 1, pl.ds(0, 3)], b_send.at[block])
+            wait(bbuf.at[block, :, 1, 0, 0, pl.ds(0, 3)], b_send.at[block])
+            wait(bbuf.at[block, :, 1, 0, 1], b_send.at[block])
+
+        @pl.when(core != part)
         def _():
             wait(bbuf.at[block], b_send.at[block])
 
-    send_bias(0)
+    for block in range(2):
+        group = 4 * lax.rem(flip + block, 2)
+        bias = jnp.zeros((16, HALF), F32)
+        for k in range(4):
+            slot = group + k
+            normed = []
+            for t in range(2):
+                xn = xs[pl.ds(8 * t + slot, 128, stride=16)].T.astype(BF16)
+                update = dot(xn, tri_out_ref[...])
+                v = prow[slot, 2 * t : 2 * t + 2].reshape(128, C).astype(F32)
+                first = (v + tg[slot, 128 * t : 128 * (t + 1)] * update).astype(BF16)
+                z1[slot, 128 * t : 128 * (t + 1)] = first
+                normed.append(layer_norm(first.astype(F32)).astype(BF16))
+            normed = jnp.concatenate(normed, axis=0)
+            yn[core, slot] = normed
+            weights = jnp.where(lax.rem(row_id, 4) == k, columns, 0.0).astype(BF16)
+            bias += dot_t(weights, normed)
+        for t in range(2):
+            bmsg[block, t] = bias[:, 128 * t : 128 * (t + 1)].astype(BF16)
+        if block == 0:
+            spread(0)
+        rows = yn.at[core, pl.ds(group, 4)]
+        push(rows, rows, yn_sem.at[0], yn_sem.at[1], (r + 1 - 2 * core, q))
 
     sub_id = lax.broadcasted_iota(jnp.int32, (128, C), 0)
     upper = lax.rem(sub_id, 8) < 4
@@ -304,7 +301,7 @@
         return carry
 
     lax.fori_loop(0, OWN, own_qkvg, 0)
-    share.wait()
+    wait(yn.at[0], yn_sem.at[1])
 
     def other_kv(s, carry):
         kv = dot(yn[1 - core, s], qkvg_ref[:, C : 3 * C])
@@ -313,17 +310,25 @@
         return carry
 
     lax.fori_loop(0, OWN, other_kv, 0)
-    bias_sent(0)
-    send_bias(1)
+
+    def multiply(block):
+        def one(s, carry):
+            raw[block, s] = dot_t(qx[block, s], kb[:, s].reshape(2 * HALF, C))
+            return carry
+
+        lax.fori_loop(0, OWN, one, 0)
+
+    multiply(0)
+    spread_done(0)
+    spread(1)
+    multiply(1)
 
     key_id = lax.broadcasted_iota(jnp.int32, (1, 2 * HALF), 1)
     key_bias = jnp.where(key_id < limit, 0.0, -1000000000.0).astype(F32)
 
     def attend(block, s):
-        keys = kb[:, s].reshape(2 * HALF, C)
         vals = vb[:, s].reshape(2 * HALF, C)
-        bias = jnp.concatenate([bbuf[block, 0], bbuf[block, 1]], axis=-1)
-        scores = dot_t(qx[block, s], keys) + (bias.reshape(512, 2 * HALF).astype(F32) + key_bias)
+        scores = raw[block, s] + full_bias[...]
         expo = jnp.exp(scores - jnp.max(scores, axis=-1, keepdims=True))
         total = jnp.sum(expo, axis=-1, keepdims=True)
         got = (dot(expo.astype(BF16), vals) / total).reshape(16, 2, 2, 8, C) * head_mask
@@ -335,6 +340,8 @@
 
     for block in range(2):
         wait(bbuf.at[block], b_recv.at[block])
+        tiles = [bbuf[block, t, c].reshape(512, 128) for c in range(2) for t in range(2)]
+        full_bias[...] = jnp.concatenate(tiles, axis=-1).astype(F32) + key_bias
 
         def finish(s, carry, block=block):
             gate = ag[s].reshape(4, 2, 32, C)[:, block].reshape(128, C)
@@ -364,7 +371,8 @@
         wait(prow, pair_sem.at[0])
         wait(prow, o_sem.at[0])
 
-    bias_sent(1)
+    wait(yn.at[0], yn_sem.at[0])
+    spread_done(1)
     wait(out_ref, o_sem.at[1])
 
 
@@ -398,13 +406,15 @@
             pltpu.VMEM((OWN, HALF, C), F32),
             pltpu.VMEM((OWN, HALF, C), BF16),
             pltpu.VMEM((2, OWN, HALF, C), BF16),
-            pltpu.VMEM((2, 16, HALF), BF16),
-            pltpu.VMEM((2, 2, N_CHIP // 2, 16, HALF), BF16),
+            pltpu.VMEM((2, 2, 16, 128), BF16),
+            pltpu.VMEM((2, 2, 2, 4, 2, 4, 16, 128), BF16),
             pltpu.VMEM((2, OWN, 512, C), BF16),
             pltpu.VMEM((2, OWN, HALF, C), BF16),
             pltpu.VMEM((2, OWN, HALF, C), BF16),
             pltpu.VMEM((OWN, HALF, C), F32),
             pltpu.VMEM((OWN, 4, COLS, C), BF16),
+            pltpu.VMEM((512, 2 * HALF), F32),
+            pltpu.VMEM((2, OWN, 512, 2 * HALF), F32),
             dma((7,)),
             pltpu.SemaphoreType.REGULAR,
             dma((2,)),

time: 69.5 us -> 67.6 us (0.973)
  Pallas kernels: 66.8 us -> 64.9 us
    pallas_call x1, Pallas kernels: 66.8 us -> 64.9 us  [local(): pl.pallas_call(kernel, out_shape=jax.ShapeDtypeStruct(pair.shape, pair.dt...]
where the time goes in v6:
time: 67.6 us; the launch traced here: 67.5 us
  Pallas kernels  64.9 us (96%)
  local copies, waits for them, and re-layouts  1.87 us (3%)
    pallas_call x1, Pallas kernels, local(): pl.pallas_call(kernel, out_shape=jax.ShapeDtypeStruct(pair.shape, pair.dt...  64.9 us
    unnamed x1, local copies, waits for them, and re-layouts  1.87 us

profile of v6, /device:TPU:1, one launch (start us, length us, event | category | flops | bytes accessed | tf_op | source)
XLA Modules:
  0.0 67.5 jit_solution(16931870755051810478)
XLA Ops:
  0.7 64.9 %pairformer.1 = bf16[32,64,128]{2,1,0:T(8,128)(2,1)} custom-call(bf16[32,64,128]{2,1,0:T(8,128)(2,1)} %pair_ref.1, s32[1]{0:T(128)S(6)} %copy.10.limit_ref, bf16[128,512]{1,0:T(8,128)(2,1)} %tri_in_hbm.1, bf16[128,128]{1,0:T(8,128)(2,1)} %tri_gate_hbm.1, bf16[128,128]{1,0:T(8,128)(2,1)} %tri_out_hbm.1, bf16[128,512]{1,0:T(8,128)(2,1)} %qkvg_hbm.1, ...), custom_call_target="tpu_custom_call" | custom-call | tf_op jit(solution)/shard_map/pairformer/pallas_call | solution.py:383
  65.6 1.9 %copy.11 = bf16[32,64,128]{2,1,0:T(8,128)(2,1)} copy(bf16[32,64,128]{2,1,0:T(8,128)(2,1)} %pairformer.1) | data formatting | bytes 1048576

commit v7 on v6

--- a/solution.py
+++ b/solution.py
@@ -377,7 +377,11 @@
 
 
 def local(pair, valid_len, tri_in, tri_gate, tri_out, att_qkvg, att_bias, att_out):
-    hbm = pl.BlockSpec(memory_space=pltpu.HBM)
+    hbm = pl.BlockSpec(memory_space=pl.ANY)
+
+    def hold(array):
+        return pltpu.with_memory_space_constraint(array, pltpu.HBM)
+
     smem = pl.BlockSpec(memory_space=pltpu.SMEM)
     dma = pltpu.SemaphoreType.DMA
     return pl.pallas_call(
@@ -426,10 +430,10 @@
             dma((2,)),
         ],
         compiler_params=pltpu.CompilerParams(
-            collective_id=0, has_side_effects=True, vmem_limit_bytes=63 * 2**20
+            collective_id=0, has_side_effects=True, vmem_limit_bytes=52 * 2**20
         ),
         name="pairformer",
-    )(pair, valid_len, tri_in, tri_gate, tri_out, att_qkvg, att_bias.T, att_out)
+    )(hold(pair), valid_len, hold(tri_in), hold(tri_gate), hold(tri_out), hold(att_qkvg), hold(att_bias.T), hold(att_out))
 
 
 def solution(mesh):

time: 67.6 us -> 66.5 us (0.984)
  local copies, waits for them, and re-layouts: 1.87 us -> 0.8 us
    unnamed x1, local copies, waits for them, and re-layouts: 1.87 us -> 0.8 us
where the time goes in v7:
time: 66.5 us; the launch traced here: 66.4 us
  Pallas kernels  64.9 us (98%)
  local copies, waits for them, and re-layouts  0.8 us (1%)
    pallas_call x1, Pallas kernels, local(): pl.pallas_call(kernel, out_shape=jax.ShapeDtypeStruct(pair.shape, pair.dt...  64.9 us

profile of v7, /device:TPU:1, one launch (start us, length us, event | category | flops | bytes accessed | tf_op | source)
XLA Modules:
  0.0 66.4 jit_solution(9543938965249577656)
XLA Ops:
  0.7 64.9 %pairformer.1 = bf16[32,64,128]{2,1,0:T(8,128)(2,1)S(1)} custom-call(bf16[32,64,128]{2,1,0:T(8,128)(2,1)} %pair_ref.1, s32[1]{0:T(128)S(6)} %copy.10.limit_ref, bf16[128,512]{1,0:T(8,128)(2,1)} %tri_in_hbm.1, bf16[128,128]{1,0:T(8,128)(2,1)} %tri_gate_hbm.1, bf16[128,128]{1,0:T(8,128)(2,1)} %tri_out_hbm.1, bf16[128,512]{1,0:T(8,128)(2,1)} %qkvg_hbm.1, ...), custom_call_target="tpu_custom_call" | custom-call | tf_op jit(solution)/shard_map/pairformer/pallas_call | solution.py:387
  65.6 0.8 %copy.11 = bf16[32,64,128]{2,1,0:T(8,128)(2,1)} copy(bf16[32,64,128]{2,1,0:T(8,128)(2,1)S(1)} %pairformer.1) | data formatting | bytes 1048576

commit v8 on v7

--- a/solution.py
+++ b/solution.py
@@ -130,7 +130,6 @@
         return carry
 
     lax.fori_loop(0, 8, norm_block, 0)
-    pl.semaphore_wait(in_sem, len(peers))
 
     s_id = lax.broadcasted_iota(jnp.int32, (16, 128), 0)
     l_id = lax.broadcasted_iota(jnp.int32, (16, 128), 1)
@@ -169,6 +168,11 @@
         lax.fori_loop(0, 4, gate, 0)
         both = stage[...].reshape(32, 2, 16, 128) * mask
         amsg[pl.ds(first, 32)] = both.astype(BF16)
+
+        @pl.when(n == 0)
+        def _():
+            pl.semaphore_wait(in_sem, len(peers))
+
 
         for dx, dy in planes:
             tx, ty = xs_at[dx], ys_at[dy]

time: 66.5 us -> 66.5 us (level)
  no operation moved by 1% of the time
where the time goes in v8:
time: 66.5 us; the launch traced here: 66.4 us
  Pallas kernels  64.9 us (98%)
  local copies, waits for them, and re-layouts  0.8 us (1%)
    pallas_call x1, Pallas kernels, local(): pl.pallas_call(kernel, out_shape=jax.ShapeDtypeStruct(pair.shape, pair.dt...  64.9 us

profile of v8, /device:TPU:1, one launch (start us, length us, event | category | flops | bytes accessed | tf_op | source)
XLA Modules:
  0.0 66.4 jit_solution(4442073729493696471)
XLA Ops:
  0.7 64.9 %pairformer.1 = bf16[32,64,128]{2,1,0:T(8,128)(2,1)S(1)} custom-call(bf16[32,64,128]{2,1,0:T(8,128)(2,1)} %pair_ref.1, s32[1]{0:T(128)S(6)} %copy.10.limit_ref, bf16[128,512]{1,0:T(8,128)(2,1)} %tri_in_hbm.1, bf16[128,128]{1,0:T(8,128)(2,1)} %tri_gate_hbm.1, bf16[128,128]{1,0:T(8,128)(2,1)} %tri_out_hbm.1, bf16[128,512]{1,0:T(8,128)(2,1)} %qkvg_hbm.1, ...), custom_call_target="tpu_custom_call" | custom-call | tf_op jit(solution)/shard_map/pairformer/pallas_call | solution.py:391
  65.6 0.8 %copy.11 = bf16[32,64,128]{2,1,0:T(8,128)(2,1)} copy(bf16[32,64,128]{2,1,0:T(8,128)(2,1)S(1)} %pairformer.1) | data formatting | bytes 1048576
